TPU v7x, 512 devices: a whole 4x4x16 slice. The times are simulated.
512 devices in a mesh: patch: 128 (over x_hi, y, z), head: 4 (over x_lo, core).
Axes of the slice: x: 4 (x_hi: 2, x_lo: 2; x = x_hi * 2 + x_lo), y: 4, z: 16, core: 2. Of those that a mesh axis runs over, the one named last changes fastest.
Arguments:
- latents: bfloat16 [16384, 1536], P('patch', 'head'), may hold values from -6 to 6
- timestep: int32 [1], replicated, may hold values from 0 to 999
- conv_weight: float32 [3, 1536], P(None, 'head'), may hold values from -3 to 3
- norm_gain: float32 [1536], replicated, may hold values from 0.1 to 1.9
- ada_gain: float32 [1536], replicated, may hold values from -4 to 4
- w_query: bfloat16 [1536, 2560], P(None, 'head'), may hold values from -0.15625 to 0.15625
- w_kv: bfloat16 [2, 1536, 512], P(None, None, 'head'), may hold values from -0.375 to 0.375
- w_out: bfloat16 [2560, 1536], P('head'), may hold values from -0.125 to 0.125
- stale_kv: bfloat16 [2, 16384, 512], P(None, 'patch', 'head'), may hold values from -280 to 280
Outputs:
- denoised: bfloat16 [16384, 1536], P('patch', 'head')
- fresh_kv: bfloat16 [2, 16384, 512], P(None, 'patch', 'head')
All inputs are finite; a program needn't handle non-finite values.
Results may differ from a plain program's by a relative error of at most 0.024.
The roundings to bfloat16 on the way count: a program that leaves them out, or rounds other values in their place, can miss the bound.
Values may be sent and summed in bfloat16 or wider, within the bound.
No kernel may reach another device: no remote copies, remote signals or barrier semaphores. Data moves between devices by JAX's collectives and lax.ppermute only.
A program may use at most 64 MiB of HBM per device.

v0:
```python
import math

import jax
import jax.numpy as jnp
from jax import lax
from jax.sharding import PartitionSpec as P

NEG_BIG = -1e30
EPS_NORM = 1e-06
MAX_BLOCK = 2048


def with_halo(value, sides, width):
    for axis, dim in sides:
        peers, length = (lax.axis_size(axis), value.shape[dim])
        up = [(i, (i + 1) % peers) for i in range(peers - 1)]
        down = [(j, i) for i, j in up]
        last = lax.slice_in_dim(value, length - width, length, axis=dim)
        leading = lax.slice_in_dim(value, 0, width, axis=dim)
        before = lax.ppermute(last, axis, up)
        after = lax.ppermute(leading, axis, down)
        value = jnp.concatenate([before, value, after], axis=dim)
    return value


def embed(timestep, width):
    half_width = width // 2
    channel = jnp.arange(width, dtype=jnp.int32)
    freq_row = jnp.exp(-math.log(10000.0) * (channel % half_width).astype(jnp.float32) / half_width)
    phases = timestep.astype(jnp.float32)[0] * freq_row
    return jnp.where(channel < half_width, jnp.sin(phases), jnp.cos(phases))


def attend(state_now, query_rows, keys_blk, values_blk, own_mask, inv_root):
    run_max, run_sum, run_acc = state_now
    scores = (
        jnp.einsum("rd,nd->rn", query_rows, keys_blk, preferred_element_type=jnp.float32) * inv_root
        + own_mask[None, :]
    )
    new_max = jnp.maximum(run_max, jnp.max(scores, axis=1))
    shrink = jnp.exp(run_max - new_max)
    weights = jnp.exp(scores - new_max[:, None])
    run_sum = run_sum * shrink + jnp.sum(weights, axis=1)
    run_acc = run_acc * shrink[:, None] + jnp.dot(
        weights.astype(jnp.bfloat16), values_blk, preferred_element_type=jnp.float32
    )
    return (new_max, run_sum, run_acc)


def sweep(state_now, cache_part, begin_at, query_rows, own_begin, own_len, inv_root):
    length = cache_part.shape[1]
    block_len = math.gcd(length, MAX_BLOCK)

    def one_turn(turn_at, state_in):
        offset = turn_at * block_len
        key_value = lax.dynamic_slice_in_dim(cache_part, offset, block_len, 1)
        position = begin_at + offset + jnp.arange(block_len, dtype=jnp.int32)
        inside = (position >= own_begin) & (position < own_begin + own_len)
        own_mask = jnp.where(inside, NEG_BIG, 0.0).astype(jnp.float32)
        return attend(state_in, query_rows, key_value[0], key_value[1], own_mask, inv_root)

    return lax.fori_loop(0, length // block_len, one_turn, state_now)


def per_device(latents, timestep, conv_weight, norm_gain, ada_gain, w_query, w_kv, w_out, stale_kv):
    rows_here = latents.shape[0]
    width_local = latents.shape[1]
    rimmed = with_halo(latents, (("patch", 0),), 1).astype(jnp.float32)
    centre = rimmed[1:-1]
    stem_out = (
        centre
        + conv_weight[0] * rimmed[:-2]
        + conv_weight[1] * centre
        + conv_weight[2] * rimmed[2:]
    ).astype(jnp.bfloat16)
    gathered = lax.all_gather(stem_out, "head", axis=1, tiled=True).astype(jnp.float32)
    inv_rms = lax.rsqrt(jnp.mean(gathered * gathered, axis=1, keepdims=True) + EPS_NORM)
    modulate = norm_gain * (1.0 + 0.3 * ada_gain * embed(timestep, gathered.shape[1]))
    normed = (gathered * inv_rms * modulate).astype(jnp.bfloat16)
    queries = jnp.dot(normed, w_query, preferred_element_type=jnp.float32).astype(jnp.bfloat16)
    fresh_kv = jnp.einsum("td,kde->kte", normed, w_kv, preferred_element_type=jnp.float32).astype(
        jnp.bfloat16
    )
    head_dim = fresh_kv.shape[2]
    per_group = queries.shape[1] // head_dim
    query_rows = queries.reshape(rows_here * per_group, head_dim)
    inv_root = 1.0 / math.sqrt(head_dim)
    row_count = rows_here * per_group
    state_now = (
        jnp.full((row_count,), NEG_BIG, jnp.float32),
        jnp.zeros((row_count,), jnp.float32),
        jnp.zeros((row_count, head_dim), jnp.float32),
    )
    state_now = attend(
        state_now,
        query_rows,
        fresh_kv[0],
        fresh_kv[1],
        jnp.zeros((rows_here,), jnp.float32),
        inv_root,
    )
    own_begin = lax.axis_index("patch") * rows_here
    cache_all = lax.all_gather(stale_kv, "patch", axis=1, tiled=True)
    state_now = sweep(state_now, cache_all, 0, query_rows, own_begin, rows_here, inv_root)
    attended = (
        (state_now[2] / state_now[1][:, None])
        .astype(jnp.bfloat16)
        .reshape(rows_here, per_group * head_dim)
    )
    partial_out = jnp.dot(attended, w_out, preferred_element_type=jnp.float32)
    summed = lax.psum(partial_out.astype(jnp.bfloat16), "head").astype(jnp.float32)
    own_cols = lax.dynamic_slice_in_dim(
        summed, lax.axis_index("head") * width_local, width_local, 1
    )
    denoised = (stem_out.astype(jnp.float32) + own_cols).astype(jnp.bfloat16)
    return (denoised, fresh_kv)


def solution(mesh):
    return jax.shard_map(
        per_device,
        mesh=mesh,
        in_specs=(
            P("patch", "head"),
            P(),
            P(None, "head"),
            P(),
            P(),
            P(None, "head"),
            P(None, None, "head"),
            P("head", None),
            P(None, "patch", "head"),
        ),
        out_specs=(P("patch", "head"), P(None, "patch", "head")),
        check_vma=False,
    )
```

profile of v0, /device:TPU:1, one launch (start us, length us, event | category | flops | bytes accessed | tf_op | source)
XLA Modules:
  0.0 371.3 jit_solution(8144840886566009218)
XLA Ops:
  8.7 4.4 %collective-permute-start = (bf16[1,384]{1,0:T(2,128)(2,1)S(1)}, bf16[1,384]{1,0:T(2,128)(2,1)S(1)}, u32[]{:S(2)}, u32[]{:S(2)}) collective-permute-start(bf16[1,384]{1,0:T(2,128)(2,1)S(1)} %get-tuple-element.185), channel_id=1, source_target_pairs={{0,4},{4,8},{8,12},{12,16},{16,20},{20,24},{24,28},{28,32},{32,36}... | collective-permute-start | bytes 2312 | tf_op jit(solution)/shard_map/ppermute | solution.py:20
  13.0 1.3 collective-permute-start.1
  18.6 10.7 %all_gather.6 = bf16[128,1536]{1,0:T(8,128)(2,1)S(1)} all-gather(bf16[128,384]{1,0:T(8,128)(2,1)S(1)} %fusion.24), channel_id=1, replica_groups=mesh['patch'=128,'head'=4] {'head'}, dimensions={1}, use_global_device_ids=true | all-gather | bytes 491520 | tf_op jit(solution)/shard_map/all_gather | solution.py:76
  29.5 2.1 convolution_convert_fusion.1
  31.7 1.5 fusion.16
  33.7 223.1 %all-gather.2.cloned.1.call-done = bf16[2,16384,128]{2,1,0:T(8,128)(2,1)} async-done(((bf16[2,128,128]{2,1,0:T(8,128)(2,1)}), bf16[2,16384,128]{2,1,0:T(8,128)(2,1)}) %all-gather.2.cloned.1.call-update) | async-done | bytes 8388624 | tf_op jit(solution)/shard_map/all_gather | solution.py:103
  256.9 48.2 %while.18 = (s32[]{:T(128)}, f32[640]{0:T(1024)S(1)}, f32[640]{0:T(1024)S(1)}, f32[640,128]{1,0:T(8,128)S(1)}, bf16[2,16384,128]{2,1,0:T(8,128)(2,1)}, /*index=5...) while((s32[]{:T(128)}, f32[640]{0:T(1024)S(1)}, ...), condition=%wide.region_6.7_spmd, body=%wide.region_3.6_spmd.sunk | while | flops 685681920 | bytes 17670352 | solution.py:62
  256.9 2.0 fusion.56
  258.9 1.2 fusion.57
  260.1 2.8 fusion.58
  262.9 2.0 fusion.56
  264.9 1.2 fusion.57
  266.1 2.8 fusion.58
  268.9 2.0 fusion.56
  270.9 1.2 fusion.57
  272.1 2.8 fusion.58
  275.0 2.0 fusion.56
  276.9 1.2 fusion.57
  278.1 2.8 fusion.58
  281.0 2.0 fusion.56
  283.0 1.2 fusion.57
  284.2 2.8 fusion.58
  287.0 2.0 fusion.56
  289.0 1.2 fusion.57
  290.2 2.8 fusion.58
  293.0 2.0 fusion.56
  296.2 2.8 fusion.58
  299.0 2.0 fusion.56
  302.2 2.8 fusion.58
  305.3 1.2 convolution_convert_fusion
  306.6 56.2 %all-reduce.2.cloned.1.call-done = bf16[128,1536]{1,0:T(8,128)(2,1)} async-done(((bf16[128,1536]{1,0:T(8,128)(2,1)}), bf16[128,1536]{1,0:T(8,128)(2,1)}) %all-reduce.2.cloned.1.call-update) | async-done | bytes 393232 | tf_op jit(solution)/shard_map/psum | solution.py:111
  362.8 1.6 add_convert_fusion
  (59 shorter events, 8.8 us)
Async XLA Ops:
  7.2 298.2 %copy-start = (bf16[640,1536]{1,0:T(8,128)(2,1)S(1)}, bf16[640,1536]{1,0:T(8,128)(2,1)}, u32[]{:S(2)}) copy-start(bf16[640,1536]{1,0:T(8,128)(2,1)} %param.18) | copy-start | bytes 5898244
  7.2 249.7 %all-gather.2.cloned.1.call-start = ((), (), s32[]{:S(2)}) async-start(), calls=%async_computation | async-start | bytes 8454144 | tf_op jit(solution)/shard_map/all_gather | solution.py:103
  7.9 354.9 %all-reduce.2.cloned.1.call-start = ((), (), s32[]{:S(2)}) async-start(), calls=%async_computation.1 | async-start | bytes 786432 | tf_op jit(solution)/shard_map/psum | solution.py:111
  8.7 7.9 %collective-permute-start = (bf16[1,384]{1,0:T(2,128)(2,1)S(1)}, bf16[1,384]{1,0:T(2,128)(2,1)S(1)}, u32[]{:S(2)}, u32[]{:S(2)}) collective-permute-start(bf16[1,384]{1,0:T(2,128)(2,1)S(1)} %get-tuple-element.185), channel_id=1, source_target_pairs={{0,4},{4,8},{8,12},{12,16},{16,20},{20,24},{24,28},{28,32},{32,36}... | collective-permute-start | bytes 2312 | tf_op jit(solution)/shard_map/ppermute | solution.py:20
  13.0 4.5 %collective-permute-start.1 = (bf16[1,384]{1,0:T(2,128)(2,1)S(1)}, bf16[1,384]{1,0:T(2,128)(2,1)S(1)}, u32[]{:S(2)}, u32[]{:S(2)}) collective-permute-start(bf16[1,384]{1,0:T(2,128)(2,1)S(1)} %get-tuple-element.186), channel_id=1, source_target_pairs={{4,0},{8,4},{12,8},{16,12},{20,16},{24,20},{28,24},{32,28},{36,32}... | collective-permute-start | bytes 2312 | tf_op jit(solution)/shard_map/ppermute | solution.py:21
  33.1 223.7 %copy-start.1 = (bf16[2,128,128]{2,1,0:T(8,128)(2,1)}, bf16[2,128,128]{2,1,0:T(8,128)(2,1)S(1)}, u32[]{:S(2)}) copy-start(bf16[2,128,128]{2,1,0:T(8,128)(2,1)S(1)} %fusion.16) | copy-start | bytes 196612
Sparse Core Ops, SparseCore 0:
  12.4 244.4 all-gather.1
  306.7 56.0 all-reduce.1
where the time goes:
time: 372 us; the launch traced here: 371 us
  waiting for transfers between devices  281 us (76%)
  matrix products  43.1 us (12%)
  between operations  14.8 us (4%)
  other arithmetic  13.5 us (4%)
  blocking collectives  10.7 us (3%)
  starting transfers between devices  5.73 us (2%)
    all_gather x1, waiting for transfers between devices, per_device(): cache_all = lax.all_gather(stale_kv, 'patch', axis=1, tiled=True)  223 us
    psum x1, waiting for transfers between devices, per_device(): lax.psum(partial_out.astype(jnp.bfloat16), 'head').astype(jnp.float32)  56.2 us
    dot_general x9, matrix products, attend(): jnp.dot(weights.astype(jnp.bfloat16), values_blk, preferred_element_type=...  22.5 us
    dot_general x9, matrix products, attend(): jnp.einsum('rd,nd->rn', query_rows, keys_blk, preferred_element_type=jnp....  15.9 us
    all_gather x1, blocking collectives, per_device(): lax.all_gather(stem_out, 'head', axis=1, tiled=True).astype(jnp.float32)  10.7 us
    reduce_sum x9, other arithmetic, attend(): run_sum = run_sum * shrink + jnp.sum(weights, axis=1)  9.58 us
  transfers between devices with their start and end apart: 4, of which 3 were waited for; matrix products, arithmetic and copies ran while one was open for 2% of the time, Pallas kernels for 0%

commit v1 on v0

v1 whole, which is shorter than its diff:
```python
import functools
import math

import jax
import jax.numpy as jnp
from jax import lax
from jax.experimental import pallas as pl
from jax.experimental.pallas import tpu as pltpu
from jax.sharding import Mesh, PartitionSpec as P

EPS_NORM = 1e-06
HD = 128
GROUP = 5
TOK = 128
PEERS = 8
RING = 16
KEYS = RING * TOK
COLS = GROUP * HD
PAY = COLS + 128
LOG2_SCALE = math.log2(math.e) / math.sqrt(HD)
NT = (((1,), (1,)), ((), ()))
VMEM_LIMIT = 48 * 2**20


def embed(timestep, width):
    half_width = width // 2
    channel = jnp.arange(width, dtype=jnp.int32)
    freq_row = jnp.exp(-math.log(10000.0) * (channel % half_width).astype(jnp.float32) / half_width)
    phases = timestep.astype(jnp.float32)[0] * freq_row
    return jnp.where(channel < half_width, jnp.sin(phases), jnp.cos(phases))


def from_z(value, offset):
    return lax.ppermute(value, "z", [((i + offset) % RING, i) for i in range(RING)])


def gather_ring(kv):
    own = kv[None]
    up = from_z(own, 1)
    down = from_z(own, -1)
    parts = [up, down]
    up = from_z(jnp.concatenate([own, up]), 2)
    down = from_z(jnp.concatenate([own, down]), -2)
    parts += [up, down]
    for _ in range(2):
        up, down = from_z(up, 2), from_z(down, -2)
        parts += [up, down]
    parts.append(from_z(up[1:], 1))
    return parts


def attend_kernel(me_ref, q_ref, fresh_ref, *refs):
    del me_ref
    parts, (o_ref, k_s, v_s, s_s) = refs[:-4], refs[-4:]
    step = pl.program_id(0)

    @pl.when(step == 0)
    def _():
        row = 0
        for part in parts:
            for b in range(part.shape[0]):
                k_s[row : row + TOK, :] = part[b, 0]
                v_s[row : row + TOK, :HD] = part[b, 1]
                row += TOK
        v_s[:, HD:] = jnp.ones((KEYS, HD), jnp.bfloat16)

    @pl.when(step == PEERS - 1)
    def _():
        k_s[:TOK, :] = fresh_ref[0]
        v_s[:TOK, :HD] = fresh_ref[1]

    lane = lax.broadcasted_iota(jnp.int32, (TOK, 128), 1)
    extra = jnp.zeros((TOK, 128), jnp.float32)
    chunk = 512
    for h in range(GROUP):
        q = q_ref[0, :, h * HD : (h + 1) * HD]
        top = None
        for c in range(0, KEYS, chunk):
            s = lax.dot_general(q, k_s[c : c + chunk, :], NT, preferred_element_type=jnp.float32)
            s_s[h, :, c : c + chunk] = s
            t = functools.reduce(jnp.maximum, [s[:, j : j + 128] for j in range(0, chunk, 128)])
            top = t if top is None else jnp.maximum(top, t)
        top = jnp.max(top, axis=1, keepdims=True)
        acc = None
        for c in range(0, KEYS, chunk):
            p = jnp.exp2((s_s[h, :, c : c + chunk] - top) * LOG2_SCALE).astype(jnp.bfloat16)
            a = jnp.dot(p, v_s[c : c + chunk, :], preferred_element_type=jnp.float32)
            acc = a if acc is None else acc + a
        total = acc[:, HD:]
        o_ref[0, :, h * HD : (h + 1) * HD] = (acc[:, :HD] / total).astype(jnp.bfloat16)
        lse = top * LOG2_SCALE + jnp.log2(total)
        hi = lse.astype(jnp.bfloat16).astype(jnp.float32)
        mid = (lse - hi).astype(jnp.bfloat16).astype(jnp.float32)
        low = lse - hi - mid
        for n, term in enumerate((hi, mid, low)):
            extra = jnp.where(lane == 3 * h + n, term, extra)
    o_ref[0, :, COLS:] = extra.astype(jnp.bfloat16)


def attend(me, queries, fresh, parts):
    whole = lambda a: pl.BlockSpec(a.shape, lambda i, me_ref: (0,) * a.ndim)
    at = lambda i, me_ref: ((me_ref[0] + 1 + i) % PEERS, 0, 0)
    return pl.pallas_call(
        attend_kernel,
        grid_spec=pltpu.PrefetchScalarGridSpec(
            num_scalar_prefetch=1,
            grid=(PEERS,),
            in_specs=[pl.BlockSpec((1, TOK, COLS), at), whole(fresh)] + [whole(p) for p in parts],
            out_specs=pl.BlockSpec((1, TOK, PAY), at),
            scratch_shapes=[
                pltpu.VMEM((KEYS, HD), jnp.bfloat16),
                pltpu.VMEM((KEYS, 2 * HD), jnp.bfloat16),
                pltpu.VMEM((GROUP, TOK, KEYS), jnp.float32),
            ],
        ),
        out_shape=jax.ShapeDtypeStruct((PEERS, TOK, PAY), jnp.bfloat16),
        compiler_params=pltpu.CompilerParams(vmem_limit_bytes=VMEM_LIMIT),
        cost_estimate=pl.CostEstimate(flops=6 * 10**9, bytes_accessed=4 * 10**6, transcendentals=10**7),
    )(me, queries, fresh, *parts)


def merge_kernel(parts_ref, w_ref, o_ref):
    cols = []
    for h in range(GROUP):
        lses = []
        for j in range(PEERS):
            e = parts_ref[j, :, COLS:].astype(jnp.float32)
            lses.append(e[:, 3 * h : 3 * h + 1] + e[:, 3 * h + 1 : 3 * h + 2] + e[:, 3 * h + 2 : 3 * h + 3])
        top = functools.reduce(jnp.maximum, lses)
        total, acc = 0.0, 0.0
        for j in range(PEERS):
            w = jnp.exp2(lses[j] - top)
            total += w
            acc += w * parts_ref[j, :, h * HD : (h + 1) * HD].astype(jnp.float32)
        cols.append((acc / total).astype(jnp.bfloat16))
    attended = jnp.concatenate(cols, axis=1)
    o_ref[...] = jnp.dot(attended, w_ref[...], preferred_element_type=jnp.float32).astype(jnp.bfloat16)


def merge(parts, w_out):
    return pl.pallas_call(
        merge_kernel,
        out_shape=jax.ShapeDtypeStruct((TOK, w_out.shape[1]), jnp.bfloat16),
        compiler_params=pltpu.CompilerParams(vmem_limit_bytes=VMEM_LIMIT),
    )(parts, w_out)


def per_device(latents, timestep, conv_weight, norm_gain, ada_gain, w_query, w_kv, w_out, stale_kv):
    width = latents.shape[1]
    line = ("xh", "y", "z")
    n = 128
    up = [(i, i + 1) for i in range(n - 1)]
    before = lax.ppermute(latents[-1:], line, up)
    after = lax.ppermute(latents[:1], line, [(j, i) for i, j in up])
    kv_parts = [stale_kv[None]] + gather_ring(stale_kv)
    rimmed = jnp.concatenate([before, latents, after], axis=0).astype(jnp.float32)
    centre = rimmed[1:-1]
    stem = (
        centre + conv_weight[0] * rimmed[:-2] + conv_weight[1] * centre + conv_weight[2] * rimmed[2:]
    ).astype(jnp.bfloat16)
    gathered = lax.all_gather(stem, "head", axis=1, tiled=True).astype(jnp.float32)
    inv_rms = lax.rsqrt(jnp.mean(gathered * gathered, axis=1, keepdims=True) + EPS_NORM)
    modulate = norm_gain * (1.0 + 0.3 * ada_gain * embed(timestep, gathered.shape[1]))
    normed = (gathered * inv_rms * modulate).astype(jnp.bfloat16)
    queries = jnp.dot(normed, w_query, preferred_element_type=jnp.float32).astype(jnp.bfloat16)
    fresh = jnp.einsum("td,kde->kte", normed, w_kv, preferred_element_type=jnp.float32).astype(jnp.bfloat16)
    spread = jnp.broadcast_to(queries[None], (PEERS, TOK, COLS))
    all_queries = lax.all_to_all(spread, ("xh", "y"), 0, 0)
    me = lax.axis_index(("xh", "y")).astype(jnp.int32).reshape(1)
    partial = attend(me, all_queries, fresh, kv_parts)
    partial = lax.all_to_all(partial, ("xh", "y"), 0, 0)
    terms = merge(partial, w_out)
    terms = terms.reshape(TOK, 4, width).transpose(1, 0, 2)
    terms = lax.all_to_all(terms, "head", 0, 0)
    update = jnp.sum(terms.astype(jnp.float32), axis=0)
    denoised = (stem.astype(jnp.float32) + update).astype(jnp.bfloat16)
    return (denoised, fresh)


def solution(mesh):
    fine = Mesh(mesh.devices.reshape(2, 4, RING, 4), ("xh", "y", "z", "head"))
    patch = ("xh", "y", "z")
    return jax.shard_map(
        per_device,
        mesh=fine,
        in_specs=(
            P(patch, "head"),
            P(),
            P(None, "head"),
            P(),
            P(),
            P(None, "head"),
            P(None, None, "head"),
            P("head", None),
            P(None, patch, "head"),
        ),
        out_specs=(P(patch, "head"), P(None, patch, "head")),
        check_vma=False,
    )
```

time: 372 us -> 151 us (0.41)
  waiting for transfers between devices: 281 us -> 4.83 us
  starting transfers between devices: 5.73 us -> 56.5 us
  blocking collectives: 10.7 us -> 52.7 us
  matrix products: 43.1 us -> 2.74 us
  Pallas kernels: 0 us -> 19.8 us
  between operations: 14.8 us -> 1.54 us
  other arithmetic: 13.5 us -> 2.73 us
  local copies, waits for them, and re-layouts: 1.85 us -> 9.44 us
    all_gather x1 -> x0, waiting for transfers between devices: 223 us -> none  [per_device(): cache_all = lax.all_gather(stale_kv, 'patch', axis=1, tiled=True)]
    psum x1 -> x0, waiting for transfers between devices: 56.2 us -> none  [per_device(): lax.psum(partial_out.astype(jnp.bfloat16), 'head').astype(jnp.float32)]
    all_to_all x0 -> x2, blocking collectives: none -> 42 us  [the longest x1 29.8 us: per_device(): partial = lax.all_to_all(partial, ('xh', 'y'), 0, 0)]
    ppermute x2 -> x11, starting transfers between devices: 5.65 us -> 45.7 us  [the longest x9 40 us: from_z(): lax.ppermute(value, 'z', [((i + offset) % RING, i) for i in range(RING)])]
    dot_general x19 -> x0, matrix products: 39.6 us -> none  [the longest x9 22.5 us: attend(): jnp.dot(weights.astype(jnp.bfloat16), values_blk, preferred_element_type=...]
    pallas_call x0 -> x2, Pallas kernels: none -> 19.8 us  [the longest x1 18.4 us: attend(): pl.pallas_call(attend_kernel, grid_spec=pltpu.PrefetchScalarGridSpec(num_...]
    all_to_all x0 -> x1, starting transfers between devices: none -> 10.8 us  [per_device(): all_queries = lax.all_to_all(spread, ('xh', 'y'), 0, 0)]
    reduce_sum x9 -> x1, other arithmetic: 9.58 us -> 0.05 us  [per_device(): update = jnp.sum(terms.astype(jnp.float32), axis=0)]
  transfers between devices with their start and end apart: 4 -> 12, of which waited for: 3 -> 6; matrix products, arithmetic and copies ran while one was open for 2% -> 3% of each run, Pallas kernels for 0% -> 0%
where the time goes in v1:
time: 151 us; the launch traced here: 150 us
  starting transfers between devices  56.5 us (37%)
  blocking collectives  52.7 us (35%)
  Pallas kernels  19.8 us (13%)
  local copies, waits for them, and re-layouts  9.44 us (6%)
  waiting for transfers between devices  4.83 us (3%)
  matrix products  2.74 us (2%)
  other arithmetic  2.73 us (2%)
  between operations  1.54 us (1%)
    ppermute x9, starting transfers between devices, from_z(): lax.ppermute(value, 'z', [((i + offset) % RING, i) for i in range(RING)])  40 us
    all_to_all x1, blocking collectives, per_device(): partial = lax.all_to_all(partial, ('xh', 'y'), 0, 0)  29.8 us
    pallas_call x1, Pallas kernels, attend(): pl.pallas_call(attend_kernel, grid_spec=pltpu.PrefetchScalarGridSpec(num_...  18.4 us
    all_to_all x1, blocking collectives, per_device(): terms = lax.all_to_all(terms, 'head', 0, 0)  12.3 us
    all_to_all x1, starting transfers between devices, per_device(): all_queries = lax.all_to_all(spread, ('xh', 'y'), 0, 0)  10.8 us
    all_gather x1, blocking collectives, per_device(): lax.all_gather(stem, 'head', axis=1, tiled=True).astype(jnp.float32)  10.7 us
    unnamed x28, local copies, waits for them, and re-layouts  5.69 us
    ppermute x1, starting transfers between devices, per_device(): before = lax.ppermute(latents[-1:], line, up)  4.36 us
  transfers between devices with their start and end apart: 12, of which 6 were waited for; matrix products, arithmetic and copies ran while one was open for 3% of the time, Pallas kernels for 0%

profile of v1, /device:TPU:1, one launch (start us, length us, event | category | flops | bytes accessed | tf_op | source)
XLA Modules:
  0.0 150.4 jit_solution(5593520284209328485)
XLA Ops:
  0.6 0.9 fusion.18
  1.5 4.4 %collective-permute-start = (bf16[1,384]{1,0:T(2,128)(2,1)S(1)}, bf16[1,384]{1,0:T(2,128)(2,1)S(1)}, u32[]{:S(2)}, u32[]{:S(2)}) collective-permute-start(bf16[1,384]{1,0:T(2,128)(2,1)S(1)} %get-tuple-element.5), channel_id=1, source_target_pairs={{0,4},{4,8},{8,12},{12,16},{16,20},{20,24},{24,28},{28,32},{32,36}... | collective-permute-start | bytes 2312 | tf_op jit(solution)/shard_map/ppermute | solution.py:153
  5.9 1.3 collective-permute-start.1
  7.8 0.8 add_multiply_fusion
  8.6 0.8 slice_reduce_fusion.2
  9.5 0.9 collective-permute-done.1
  10.4 0.9 maximum_convert_fusion
  12.1 10.7 %all_gather.3 = bf16[128,1536]{1,0:T(8,128)(2,1)S(1)} all-gather(bf16[128,384]{1,0:T(8,128)(2,1)S(1)} %fusion.6), channel_id=1, replica_groups=mesh['xh'=2,'y'=4,'z'=16,'head'=4] {'head'}, dimensions={1}, use_global_device_ids=true | all-gather | bytes 491520 | tf_op jit(solution)/shard_map/all_gather | solution.py:161
  24.6 1.2 broadcast_in_dim.4
  25.7 10.8 %all-to-all-start = ((bf16[8,128,640]{2,1,0:T(8,128)(2,1)}), bf16[8,128,640]{2,1,0:T(8,128)(2,1)S(1)}, u32[]{:S(2)}, u32[]{:S(2)}) async-start(bf16[8,128,640]{2,1,0:T(8,128)(2,1)} %broadcast_in_dim.4), calls=%async_computation | async-start | bytes 2621440 | tf_op jit(solution)/shard_map/all_to_all | solution.py:168
  36.6 1.9 %collective-permute-start.3 = (bf16[1,2,128,128]{3,2,1,0:T(8,128)(2,1)S(1)}, bf16[1,2,128,128]{3,2,1,0:T(8,128)(2,1)S(1)}, u32[]{:S(2)}, u32[]{:S(2)}) collective-permute-start(bf16[1,2,128,128]{3,2,1,0:T(8,128)(2,1)S(1)} %bitcast.18), channel_id=1, source_target_pairs={{60,0},{0,4},{4,8},{8,12},{12,16},{16,20},{20,24},{24,28},{28,32},... | collective-permute-start | bytes 196616 | tf_op jit(solution)/shard_map/ppermute | solution.py:34
  38.5 5.6 %collective-permute-start.2 = (bf16[1,2,128,128]{3,2,1,0:T(8,128)(2,1)S(1)}, bf16[1,2,128,128]{3,2,1,0:T(8,128)(2,1)S(1)}, u32[]{:S(2)}, u32[]{:S(2)}) collective-permute-start(bf16[1,2,128,128]{3,2,1,0:T(8,128)(2,1)S(1)} %bitcast.19), channel_id=1, source_target_pairs={{4,0},{8,4},{12,8},{16,12},{20,16},{24,20},{28,24},{32,28},{36,32}... | collective-permute-start | bytes 196616 | tf_op jit(solution)/shard_map/ppermute | solution.py:34
  44.2 1.2 collective-permute-done.2.refs_1_
  45.4 5.2 %collective-permute-start.4 = (bf16[2,2,128,128]{3,2,1,0:T(8,128)(2,1)S(1)}, bf16[2,2,128,128]{3,2,1,0:T(8,128)(2,1)S(1)}, u32[]{:S(2)}, u32[]{:S(2)}) collective-permute-start(bf16[2,2,128,128]{3,2,1,0:T(8,128)(2,1)S(1)} %get-tuple-element.8), channel_id=1, source_target_pairs={{8,0},{12,4},{16,8},{20,12},{24,16},{28,20},{32,24},{36,28},{40,32... | collective-permute-start | bytes 393224 | tf_op jit(solution)/shard_map/ppermute | solution.py:34
  50.6 1.9 %collective-permute-start.5 = (bf16[2,2,128,128]{3,2,1,0:T(8,128)(2,1)S(1)}, bf16[2,2,128,128]{3,2,1,0:T(8,128)(2,1)}, u32[]{:S(2)}, u32[]{:S(2)}) collective-permute-start(bf16[2,2,128,128]{3,2,1,0:T(8,128)(2,1)S(1)} %get-tuple-element.7), channel_id=1, source_target_pairs={{56,0},{60,4},{0,8},{4,12},{8,16},{12,20},{16,24},{20,28},{24,32},... | collective-permute-start | bytes 393224 | tf_op jit(solution)/shard_map/ppermute | solution.py:34
  52.5 1.2 collective-permute-done.4.refs_3_
  53.8 4.9 %collective-permute-start.6 = (bf16[2,2,128,128]{3,2,1,0:T(8,128)(2,1)S(1)}, bf16[2,2,128,128]{3,2,1,0:T(8,128)(2,1)}, u32[]{:S(2)}, u32[]{:S(2)}) collective-permute-start(bf16[2,2,128,128]{3,2,1,0:T(8,128)(2,1)S(1)} %collective-permute-done.4.refs_3_), channel_id=1, source_target_pairs={{8,0},{12,4},{16,8},{20,12},{24,16},{28,20},{32,24},{36,28},{40,32... | collective-permute-start | bytes 393224 | tf_op jit(solution)/shard_map/ppermute | solution.py:34
  59.4 1.9 %collective-permute-start.7 = (bf16[2,2,128,128]{3,2,1,0:T(8,128)(2,1)}, bf16[2,2,128,128]{3,2,1,0:T(8,128)(2,1)}, u32[]{:S(2)}, u32[]{:S(2)}) collective-permute-start(bf16[2,2,128,128]{3,2,1,0:T(8,128)(2,1)} %collective-permute-done.5.refs_4_), channel_id=1, source_target_pairs={{56,0},{60,4},{0,8},{4,12},{8,16},{12,20},{16,24},{20,28},{24,32},... | collective-permute-start | bytes 393224 | tf_op jit(solution)/shard_map/ppermute | solution.py:34
  61.3 5.5 %collective-permute-start.8 = (bf16[2,2,128,128]{3,2,1,0:T(8,128)(2,1)}, bf16[2,2,128,128]{3,2,1,0:T(8,128)(2,1)}, u32[]{:S(2)}, u32[]{:S(2)}) collective-permute-start(bf16[2,2,128,128]{3,2,1,0:T(8,128)(2,1)} %collective-permute-done.6.refs_5_), channel_id=1, source_target_pairs={{8,0},{12,4},{16,8},{20,12},{24,16},{28,20},{32,24},{36,28},{40,32... | collective-permute-start | bytes 393224 | tf_op jit(solution)/shard_map/ppermute | solution.py:34
  66.8 0.7 collective-permute-done.7.refs_6_
  67.5 1.9 %collective-permute-start.9 = (bf16[2,2,128,128]{3,2,1,0:T(8,128)(2,1)}, bf16[2,2,128,128]{3,2,1,0:T(8,128)(2,1)S(1)}, u32[]{:S(2)}, u32[]{:S(2)}) collective-permute-start(bf16[2,2,128,128]{3,2,1,0:T(8,128)(2,1)} %collective-permute-done.7.refs_6_), channel_id=1, source_target_pairs={{56,0},{60,4},{0,8},{4,12},{8,16},{12,20},{16,24},{20,28},{24,32},... | collective-permute-start | bytes 393224 | tf_op jit(solution)/shard_map/ppermute | solution.py:34
  70.1 0.8 slice.39
  70.9 11.2 %collective-permute-start.10 = (bf16[1,2,128,128]{3,2,1,0:T(8,128)(2,1)S(1)}, bf16[1,2,128,128]{3,2,1,0:T(8,128)(2,1)S(1)}, u32[]{:S(2)}, u32[]{:S(2)}) collective-permute-start(bf16[1,2,128,128]{3,2,1,0:T(8,128)(2,1)S(1)} %slice.39), channel_id=1, source_target_pairs={{4,0},{8,4},{12,8},{16,12},{20,16},{24,20},{28,24},{32,28},{36,32}... | collective-permute-start | bytes 196616 | tf_op jit(solution)/shard_map/ppermute | solution.py:34
  82.1 2.2 %fusion.fresh_ref = bf16[2,128,128]{2,1,0:T(8,128)(2,1)} fusion(bf16[2,1536,128]{2,1,0:T(8,128)(2,1)} %param.15, bf16[128,1536]{1,0:T(8,128)(2,1)} %copy-done.10, f32[1536]{0:T(1024)S(1)} %add_multiply_fusion, f32[128]{0:T(128)} %copy-done.13), kind=kOutput, calls=%fused_computation.2 | convolution fusion | flops 101482496 | bytes 1251840 | tf_op jit(solution)/shard_map/td,kde->kte/dot_general | solution.py:166
  85.0 0.9 copy-done.4
  85.9 0.9 copy-done.6
  86.8 0.8 copy-done.7
  87.6 18.4 %shard_map.104 = bf16[8,128,768]{2,1,0:T(8,128)(2,1)S(1)} custom-call(s32[1]{0:T(128)} %bitcast.me_ref, bf16[8,128,640]{2,1,0:T(8,128)(2,1)S(1)} %all-to-all-done.q_ref, bf16[2,128,128]{2,1,0:T(8,128)(2,1)S(1)} %copy-done.7, bf16[1,2,128,128]{3,2,1,0:T(8,128)(2,1)S(1)} %bitcast.21, bf16[1,2,128,128]{3,2,1,0:T(8,128)(2,1)S(1)} %collective-permute-done.2.refs_1_, ...), custom_call_target="tpu_custom_call" | custom-call | flops 6000000000 | bytes 4000000 | tf_op jit(solution)/shard_map/pallas_call | solution.py:103
  106.0 29.8 %all_to_all.15.parts_ref = bf16[8,128,768]{2,1,0:T(8,128)(2,1)S(1)} all-to-all(bf16[8,128,768]{2,1,0:T(8,128)(2,1)S(1)} %shard_map.104), channel_id=1, replica_groups=mesh['xh'=2,'y'=4,'z'=16,'head'=4] {'xh','y'}, dimensions={0} | all-to-all | bytes 3145728 | tf_op jit(solution)/shard_map/all_to_all | solution.py:171
  135.8 1.5 shard_map.105
  137.3 12.3 %all_to_all.16 = bf16[4,128,384]{2,1,0:T(8,128)(2,1)S(1)} all-to-all(bf16[4,128,384]{2,1,0:T(8,128)(2,1)S(1)} %bitcast.22), channel_id=1, replica_groups=mesh['xh'=2,'y'=4,'z'=16,'head'=4] {'head'}, dimensions={0} | all-to-all | bytes 786432 | tf_op jit(solution)/shard_map/all_to_all | solution.py:174
  149.7 0.7 add_convert_fusion
  (40 shorter events, 4.7 us)
Async XLA Ops:
  0.6 23.4 %copy-start = (bf16[1536,640]{1,0:T(8,128)(2,1)S(1)}, bf16[1536,640]{1,0:T(8,128)(2,1)}, u32[]{:S(2)}) copy-start(bf16[1536,640]{1,0:T(8,128)(2,1)} %param.14) | copy-start | bytes 5898244
  1.5 7.9 %collective-permute-start = (bf16[1,384]{1,0:T(2,128)(2,1)S(1)}, bf16[1,384]{1,0:T(2,128)(2,1)S(1)}, u32[]{:S(2)}, u32[]{:S(2)}) collective-permute-start(bf16[1,384]{1,0:T(2,128)(2,1)S(1)} %get-tuple-element.5), channel_id=1, source_target_pairs={{0,4},{4,8},{8,12},{12,16},{16,20},{20,24},{24,28},{28,32},{32,36}... | collective-permute-start | bytes 2312 | tf_op jit(solution)/shard_map/ppermute | solution.py:153
  5.9 4.5 %collective-permute-start.1 = (bf16[1,384]{1,0:T(2,128)(2,1)S(1)}, bf16[1,384]{1,0:T(2,128)(2,1)S(1)}, u32[]{:S(2)}, u32[]{:S(2)}) collective-permute-start(bf16[1,384]{1,0:T(2,128)(2,1)S(1)} %get-tuple-element.6), channel_id=1, source_target_pairs={{4,0},{8,4},{12,8},{16,12},{20,16},{24,20},{28,24},{32,28},{36,32}... | collective-permute-start | bytes 2312 | tf_op jit(solution)/shard_map/ppermute | solution.py:154
  9.4 13.5 %copy-start.11 = (f32[384]{0:T(512)}, f32[384]{0:T(512)S(1)}, u32[]{:S(2)}) copy-start(f32[384]{0:T(512)S(1)} %get-tuple-element.4) | copy-start | bytes 4612
  11.3 0.7 copy-start.8
  22.8 0.7 copy-start.10
  23.5 0.5 copy-start.13
  24.6 12.0 %copy-start.2 = (bf16[2,128,128]{2,1,0:T(8,128)(2,1)S(1)}, bf16[2,128,128]{2,1,0:T(8,128)(2,1)}, u32[]{:S(2)}) copy-start(bf16[2,128,128]{2,1,0:T(8,128)(2,1)} %param.17) | copy-start | bytes 196612
  25.7 59.2 %all-to-all-start = ((bf16[8,128,640]{2,1,0:T(8,128)(2,1)}), bf16[8,128,640]{2,1,0:T(8,128)(2,1)S(1)}, u32[]{:S(2)}, u32[]{:S(2)}) async-start(bf16[8,128,640]{2,1,0:T(8,128)(2,1)} %broadcast_in_dim.4), calls=%async_computation | async-start | bytes 2621440 | tf_op jit(solution)/shard_map/all_to_all | solution.py:168
  36.6 7.7 %collective-permute-start.3 = (bf16[1,2,128,128]{3,2,1,0:T(8,128)(2,1)S(1)}, bf16[1,2,128,128]{3,2,1,0:T(8,128)(2,1)S(1)}, u32[]{:S(2)}, u32[]{:S(2)}) collective-permute-start(bf16[1,2,128,128]{3,2,1,0:T(8,128)(2,1)S(1)} %bitcast.18), channel_id=1, source_target_pairs={{60,0},{0,4},{4,8},{8,12},{12,16},{16,20},{20,24},{24,28},{28,32},... | collective-permute-start | bytes 196616 | tf_op jit(solution)/shard_map/ppermute | solution.py:34
  38.5 6.9 %collective-permute-start.2 = (bf16[1,2,128,128]{3,2,1,0:T(8,128)(2,1)S(1)}, bf16[1,2,128,128]{3,2,1,0:T(8,128)(2,1)S(1)}, u32[]{:S(2)}, u32[]{:S(2)}) collective-permute-start(bf16[1,2,128,128]{3,2,1,0:T(8,128)(2,1)S(1)} %bitcast.19), channel_id=1, source_target_pairs={{4,0},{8,4},{12,8},{16,12},{20,16},{24,20},{28,24},{32,28},{36,32}... | collective-permute-start | bytes 196616 | tf_op jit(solution)/shard_map/ppermute | solution.py:34
  45.4 8.3 %collective-permute-start.4 = (bf16[2,2,128,128]{3,2,1,0:T(8,128)(2,1)S(1)}, bf16[2,2,128,128]{3,2,1,0:T(8,128)(2,1)S(1)}, u32[]{:S(2)}, u32[]{:S(2)}) collective-permute-start(bf16[2,2,128,128]{3,2,1,0:T(8,128)(2,1)S(1)} %get-tuple-element.8), channel_id=1, source_target_pairs={{8,0},{12,4},{16,8},{20,12},{24,16},{28,20},{32,24},{36,28},{40,32... | collective-permute-start | bytes 393224 | tf_op jit(solution)/shard_map/ppermute | solution.py:34
  50.6 8.8 %collective-permute-start.5 = (bf16[2,2,128,128]{3,2,1,0:T(8,128)(2,1)S(1)}, bf16[2,2,128,128]{3,2,1,0:T(8,128)(2,1)}, u32[]{:S(2)}, u32[]{:S(2)}) collective-permute-start(bf16[2,2,128,128]{3,2,1,0:T(8,128)(2,1)S(1)} %get-tuple-element.7), channel_id=1, source_target_pairs={{56,0},{60,4},{0,8},{4,12},{8,16},{12,20},{16,24},{20,28},{24,32},... | collective-permute-start | bytes 393224 | tf_op jit(solution)/shard_map/ppermute | solution.py:34
  53.8 7.5 %collective-permute-start.6 = (bf16[2,2,128,128]{3,2,1,0:T(8,128)(2,1)S(1)}, bf16[2,2,128,128]{3,2,1,0:T(8,128)(2,1)}, u32[]{:S(2)}, u32[]{:S(2)}) collective-permute-start(bf16[2,2,128,128]{3,2,1,0:T(8,128)(2,1)S(1)} %collective-permute-done.4.refs_3_), channel_id=1, source_target_pairs={{8,0},{12,4},{16,8},{20,12},{24,16},{28,20},{32,24},{36,28},{40,32... | collective-permute-start | bytes 393224 | tf_op jit(solution)/shard_map/ppermute | solution.py:34
  58.7 0.7 copy-start.3
  59.4 8.1 %collective-permute-start.7 = (bf16[2,2,128,128]{3,2,1,0:T(8,128)(2,1)}, bf16[2,2,128,128]{3,2,1,0:T(8,128)(2,1)}, u32[]{:S(2)}, u32[]{:S(2)}) collective-permute-start(bf16[2,2,128,128]{3,2,1,0:T(8,128)(2,1)} %collective-permute-done.5.refs_4_), channel_id=1, source_target_pairs={{56,0},{60,4},{0,8},{4,12},{8,16},{12,20},{16,24},{20,28},{24,32},... | collective-permute-start | bytes 393224 | tf_op jit(solution)/shard_map/ppermute | solution.py:34
  61.3 8.7 %collective-permute-start.8 = (bf16[2,2,128,128]{3,2,1,0:T(8,128)(2,1)}, bf16[2,2,128,128]{3,2,1,0:T(8,128)(2,1)}, u32[]{:S(2)}, u32[]{:S(2)}) collective-permute-start(bf16[2,2,128,128]{3,2,1,0:T(8,128)(2,1)} %collective-permute-done.6.refs_5_), channel_id=1, source_target_pairs={{8,0},{12,4},{16,8},{20,12},{24,16},{28,20},{32,24},{36,28},{40,32... | collective-permute-start | bytes 393224 | tf_op jit(solution)/shard_map/ppermute | solution.py:34
  67.5 16.8 %collective-permute-start.9 = (bf16[2,2,128,128]{3,2,1,0:T(8,128)(2,1)}, bf16[2,2,128,128]{3,2,1,0:T(8,128)(2,1)S(1)}, u32[]{:S(2)}, u32[]{:S(2)}) collective-permute-start(bf16[2,2,128,128]{3,2,1,0:T(8,128)(2,1)} %collective-permute-done.7.refs_6_), channel_id=1, source_target_pairs={{56,0},{60,4},{0,8},{4,12},{8,16},{12,20},{16,24},{20,28},{24,32},... | collective-permute-start | bytes 393224 | tf_op jit(solution)/shard_map/ppermute | solution.py:34
  70.9 14.1 %collective-permute-start.10 = (bf16[1,2,128,128]{3,2,1,0:T(8,128)(2,1)S(1)}, bf16[1,2,128,128]{3,2,1,0:T(8,128)(2,1)S(1)}, u32[]{:S(2)}, u32[]{:S(2)}) collective-permute-start(bf16[1,2,128,128]{3,2,1,0:T(8,128)(2,1)S(1)} %slice.39), channel_id=1, source_target_pairs={{4,0},{8,4},{12,8},{16,12},{20,16},{24,20},{28,24},{32,28},{36,32}... | collective-permute-start | bytes 196616 | tf_op jit(solution)/shard_map/ppermute | solution.py:34
  84.3 0.6 copy-start.5
  85.0 0.9 copy-start.4
  85.9 0.9 copy-start.6
  86.8 0.8 copy-start.7
  106.0 29.8 %copy-start.1 = (bf16[640,1536]{1,0:T(8,128)(2,1)S(1)}, bf16[640,1536]{1,0:T(8,128)(2,1)}, u32[]{:S(2)}) copy-start(bf16[640,1536]{1,0:T(8,128)(2,1)} %w_ref.1) | copy-start | bytes 5898244
  137.3 12.4 %copy-start.9 = (f32[130,384]{1,0:T(8,128)S(1)}, f32[130,384]{1,0:T(8,128)}, u32[]{:S(2)}) copy-start(f32[130,384]{1,0:T(8,128)} %copy-done.8) | copy-start | bytes 599044
  137.3 12.4 %copy-start.12 = (f32[384]{0:T(512)S(1)}, f32[384]{0:T(512)}, u32[]{:S(2)}) copy-start(f32[384]{0:T(512)} %copy-done.11) | copy-start | bytes 4612

commit v2 on v1

v2 whole, which is shorter than its diff:
```python
import functools
import math

import jax
import jax.numpy as jnp
from jax import lax
from jax.experimental import pallas as pl
from jax.experimental.pallas import tpu as pltpu
from jax.sharding import Mesh, PartitionSpec as P

EPS_NORM = 1e-06
HD = 128
GROUP = 5
TOK = 128
PEERS = 4
ROWS = 320
PLANE = ("xh", "zl")
COLS = GROUP * HD
PAY = COLS + 128
LOG2_SCALE = math.log2(math.e) / math.sqrt(HD)
NT = (((1,), (1,)), ((), ()))
VMEM_LIMIT = 48 * 2**20


def embed(timestep, width):
    half_width = width // 2
    channel = jnp.arange(width, dtype=jnp.int32)
    freq_row = jnp.exp(-math.log(10000.0) * (channel % half_width).astype(jnp.float32) / half_width)
    phases = timestep.astype(jnp.float32)[0] * freq_row
    return jnp.where(channel < half_width, jnp.sin(phases), jnp.cos(phases))


def swap(value, turn):
    n = lax.axis_size("zh")
    pairs = []
    for i in range(turn, n + turn, 2):
        j = (i + 1) % n
        pairs += [(i, j), (j, i)]
    return lax.ppermute(value, "zh", pairs)


def flip(value, bits):
    return lax.ppermute(value, PLANE, [(i, i ^ bits) for i in range(PEERS)])


def attend_kernel(where_ref, *refs):
    qs, (near_ref, far_ref, fresh_ref, o_ref, k_s, v_s, s_s) = refs[:PEERS], refs[PEERS:]
    keys = k_s.shape[0]
    row = 0
    for ref in (near_ref, far_ref):
        for y in range(ref.shape[0]):
            for b in range(ref.shape[1]):
                k_s[row : row + TOK, :] = ref[y, b, 0]
                v_s[row : row + TOK, :HD] = ref[y, b, 1]
                row += TOK
    v_s[:, HD:] = jnp.ones((keys, HD), jnp.bfloat16)
    for bits in range(PEERS - 1, -1, -1):
        if bits == 0:
            rows = pl.ds(pl.multiple_of(where_ref[1] * TOK, TOK), TOK)
            k_s[rows, :] = fresh_ref[0]
            v_s[rows, :HD] = fresh_ref[1]
        attend_patch(qs[bits], o_ref.at[where_ref[0] ^ bits], k_s, v_s, s_s)


def attend_patch(q_ref, o_ref, k_s, v_s, s_s):
    keys = k_s.shape[0]
    q = jnp.concatenate([q_ref[:, h * HD : (h + 1) * HD] for h in range(GROUP)], axis=0)
    chunk = 512

    def scores(r):
        top = None
        for c in range(0, keys, chunk):
            s = lax.dot_general(q[r : r + ROWS], k_s[c : c + chunk, :], NT, preferred_element_type=jnp.float32)
            s_s[r : r + ROWS, c : c + chunk] = s
            t = functools.reduce(jnp.maximum, [s[:, j : j + 128] for j in range(0, chunk, 128)])
            top = t if top is None else jnp.maximum(top, t)
        return jnp.max(top, axis=1, keepdims=True)

    def mix(r, top):
        acc = None
        for c in range(0, keys, chunk):
            p = jnp.exp2((s_s[r : r + ROWS, c : c + chunk] - top) * LOG2_SCALE).astype(jnp.bfloat16)
            a = jnp.dot(p, v_s[c : c + chunk, :], preferred_element_type=jnp.float32)
            acc = a if acc is None else acc + a
        total = acc[:, HD:]
        return acc[:, :HD] / total, top * LOG2_SCALE + jnp.log2(total)

    starts = list(range(0, COLS, ROWS))
    tops, mixed = [scores(0)], []
    for n, r in enumerate(starts):
        if n + 1 < len(starts):
            tops.append(scores(starts[n + 1]))
        mixed.append(mix(r, tops[n]))
    out, lses = (jnp.concatenate([m[i] for m in mixed], axis=0) for i in range(2))
    lane = lax.broadcasted_iota(jnp.int32, (TOK, 128), 1)
    extra = jnp.zeros((TOK, 128), jnp.float32)
    for h in range(GROUP):
        rows = slice(h * TOK, (h + 1) * TOK)
        o_ref[:, h * HD : (h + 1) * HD] = out[rows].astype(jnp.bfloat16)
        lse = lses[rows]
        hi = lse.astype(jnp.bfloat16).astype(jnp.float32)
        mid = (lse - hi).astype(jnp.bfloat16).astype(jnp.float32)
        low = lse - hi - mid
        for n, term in enumerate((hi, mid, low)):
            extra = jnp.where(lane == 3 * h + n, term, extra)
    o_ref[:, COLS:] = extra.astype(jnp.bfloat16)


def attend(where, queries, near, far, fresh):
    keys = TOK * (math.prod(near.shape[:2]) + math.prod(far.shape[:2]))
    vmem = pl.BlockSpec(memory_space=pltpu.VMEM)
    return pl.pallas_call(
        attend_kernel,
        in_specs=[pl.BlockSpec(memory_space=pltpu.SMEM)] + [vmem] * (PEERS + 3),
        out_specs=vmem,
        scratch_shapes=[
            pltpu.VMEM((keys, HD), jnp.bfloat16),
            pltpu.VMEM((keys, 2 * HD), jnp.bfloat16),
            pltpu.VMEM((COLS, keys), jnp.float32),
        ],
        out_shape=jax.ShapeDtypeStruct((PEERS, TOK, PAY), jnp.bfloat16),
        compiler_params=pltpu.CompilerParams(vmem_limit_bytes=VMEM_LIMIT),
        cost_estimate=pl.CostEstimate(
            flops=15 * 10**9, bytes_accessed=4 * 10**6, transcendentals=PEERS * COLS * keys
        ),
    )(where, *queries, near, far, fresh)


def copies_kernel(n_parts, *refs):
    parts, out_ref = refs[:n_parts], refs[-1]
    for j in range(out_ref.shape[0]):
        row = 0
        for part in parts:
            n = part.shape[0]
            out_ref[j, row : row + n] = part[...]
            row += n


def spread(parts, n, behind):
    blocks = sum(p.shape[0] for p in parts)
    vmem = pl.BlockSpec(memory_space=pltpu.VMEM)
    return pl.pallas_call(
        functools.partial(copies_kernel, len(parts)),
        in_specs=[vmem] * len(parts) + [pl.BlockSpec(memory_space=pl.ANY)],
        out_specs=vmem,
        out_shape=jax.ShapeDtypeStruct((n, blocks) + parts[0].shape[1:], jnp.bfloat16),
        compiler_params=pltpu.CompilerParams(vmem_limit_bytes=VMEM_LIMIT),
        cost_estimate=pl.CostEstimate(flops=10**5, bytes_accessed=10**6, transcendentals=0),
    )(*parts, behind)


def stem_kernel(x_ref, before_ref, after_ref, w_ref, stem_ref):
    x = x_ref[...].astype(jnp.float32)
    row = lax.broadcasted_iota(jnp.int32, x.shape, 0)
    prev = jnp.where(row == 0, before_ref[...].astype(jnp.float32), pltpu.roll(x, 1, 0))
    follow = jnp.where(row == TOK - 1, after_ref[...].astype(jnp.float32), pltpu.roll(x, TOK - 1, 0))
    stem = x + w_ref[0:1, :] * prev + w_ref[1:2, :] * x + w_ref[2:3, :] * follow
    stem_ref[...] = stem.astype(jnp.bfloat16)


def stem_of(latents, before, after, conv_weight):
    vmem = pl.BlockSpec(memory_space=pltpu.VMEM)
    return pl.pallas_call(
        stem_kernel,
        in_specs=[vmem] * 4,
        out_specs=vmem,
        out_shape=jax.ShapeDtypeStruct(latents.shape, jnp.bfloat16),
        compiler_params=pltpu.CompilerParams(vmem_limit_bytes=VMEM_LIMIT),
        cost_estimate=pl.CostEstimate(flops=10**6, bytes_accessed=10**6, transcendentals=0),
    )(latents, before, after, conv_weight)


def project_kernel(x_ref, mod_ref, wq_ref, wkv_ref, q_ref, fresh_ref):
    x = x_ref[...].astype(jnp.float32)
    inv = lax.rsqrt(jnp.mean(x * x, axis=1, keepdims=True) + EPS_NORM)
    normed = (x * inv * mod_ref[...]).astype(jnp.bfloat16)
    q_ref[...] = jnp.dot(normed, wq_ref[...], preferred_element_type=jnp.float32).astype(jnp.bfloat16)
    for i in range(2):
        fresh_ref[i] = jnp.dot(normed, wkv_ref[i], preferred_element_type=jnp.float32).astype(jnp.bfloat16)


def project(x, mod, w_query, w_kv):
    vmem = pl.BlockSpec(memory_space=pltpu.VMEM)
    return pl.pallas_call(
        project_kernel,
        in_specs=[vmem] * 4,
        out_shape=[
            jax.ShapeDtypeStruct((TOK, COLS), jnp.bfloat16),
            jax.ShapeDtypeStruct((2, TOK, HD), jnp.bfloat16),
        ],
        compiler_params=pltpu.CompilerParams(vmem_limit_bytes=VMEM_LIMIT),
        cost_estimate=pl.CostEstimate(flops=4 * 10**8, bytes_accessed=5 * 10**6, transcendentals=0),
    )(x, mod, w_query, w_kv)


def merge_kernel(parts_ref, w_ref, o_ref):
    cols = []
    for h in range(GROUP):
        lses = []
        for j in range(PEERS):
            e = parts_ref[j, :, COLS:].astype(jnp.float32)
            lses.append(e[:, 3 * h : 3 * h + 1] + e[:, 3 * h + 1 : 3 * h + 2] + e[:, 3 * h + 2 : 3 * h + 3])
        top = functools.reduce(jnp.maximum, lses)
        total, acc = 0.0, 0.0
        for j in range(PEERS):
            w = jnp.exp2(lses[j] - top)
            total += w
            acc += w * parts_ref[j, :, h * HD : (h + 1) * HD].astype(jnp.float32)
        cols.append((acc / total).astype(jnp.bfloat16))
    attended = jnp.concatenate(cols, axis=1)
    o_ref[...] = jnp.dot(attended, w_ref[...], preferred_element_type=jnp.float32).astype(jnp.bfloat16)


def merge(parts, w_out):
    return pl.pallas_call(
        merge_kernel,
        out_shape=jax.ShapeDtypeStruct((TOK, w_out.shape[1]), jnp.bfloat16),
        compiler_params=pltpu.CompilerParams(vmem_limit_bytes=VMEM_LIMIT),
    )(parts, w_out)


def per_device(latents, timestep, conv_weight, norm_gain, ada_gain, w_query, w_kv, w_out, stale_kv):
    width = latents.shape[1]
    line = ("xh", "y", "zh", "zl")
    n = 128
    up = [(i, i + 1) for i in range(n - 1)]
    before = lax.ppermute(latents[-1:], line, up)
    after = lax.ppermute(latents[:1], line, [(j, i) for i, j in up])
    own = stale_kv[None]
    got = [swap(own, 0)]
    stem = stem_of(latents, before, after, conv_weight)
    got.append(swap(spread([own] + got, 1, stem)[0], 1))
    gathered = lax.all_gather(stem, "head", axis=1, tiled=True)
    modulate = norm_gain * (1.0 + 0.3 * ada_gain * embed(timestep, gathered.shape[1]))
    near = lax.all_to_all(spread([own] + got, 4, gathered), "y", 0, 0)
    got.append(swap(got[1], 0))
    queries, fresh = project(gathered, modulate[None], w_query, w_kv)
    got.append(swap(spread(got[2:3], 1, queries)[0], 1))
    all_queries = [queries] + [flip(queries, bits) for bits in range(1, PEERS)]
    far = lax.all_to_all(spread(got[2:], 4, all_queries[1]), "y", 0, 0)
    where = jnp.stack([lax.axis_index(PLANE), 4 * lax.axis_index("y")]).astype(jnp.int32)
    partial = attend(where, all_queries, near, far, fresh)
    partial = lax.all_to_all(partial, PLANE, 0, 0)
    terms = merge(partial, w_out)
    terms = terms.reshape(TOK, 4, width).transpose(1, 0, 2)
    terms = lax.all_to_all(terms, "head", 0, 0)
    update = jnp.sum(terms.astype(jnp.float32), axis=0)
    denoised = (stem.astype(jnp.float32) + update).astype(jnp.bfloat16)
    return (denoised, fresh)


def solution(mesh):
    fine = Mesh(mesh.devices.reshape(2, 4, 8, 2, 4), ("xh", "y", "zh", "zl", "head"))
    patch = ("xh", "y", "zh", "zl")
    return jax.shard_map(
        per_device,
        mesh=fine,
        in_specs=(
            P(patch, "head"),
            P(),
            P(None, "head"),
            P(),
            P(),
            P(None, "head"),
            P(None, None, "head"),
            P("head", None),
            P(None, patch, "head"),
        ),
        out_specs=(P(patch, "head"), P(None, patch, "head")),
        check_vma=False,
    )
```

time: 151 us -> 125 us (0.83)
  blocking collectives: 52.7 us -> 37.2 us
  waiting for transfers between devices: 4.83 us -> 11.7 us
  starting transfers between devices: 56.5 us -> 49.9 us
  local copies, waits for them, and re-layouts: 9.44 us -> 5.66 us
  matrix products: 2.74 us -> 0 us
  Pallas kernels: 19.8 us -> 17.4 us
  other arithmetic: 2.73 us -> 0.86 us
    all_to_all x1, blocking collectives: 29.8 us -> 15.6 us  [per_device(): partial = lax.all_to_all(partial, PLANE, 0, 0)]
    ppermute x9 -> x7, waiting for transfers between devices: 3.9 us -> 8.68 us  [the longest x4 5.05 us: swap(): return lax.ppermute(value, 'zh', pairs)]
    ppermute x9 -> x7, starting transfers between devices: 40 us -> 37.1 us  [the longest x4 19 us: swap(): return lax.ppermute(value, 'zh', pairs)]
    all_to_all x1 -> x2, starting transfers between devices: 10.8 us -> 7.94 us  [the longest x1 4.18 us: per_device(): near = lax.all_to_all(spread([own] + got, 4, gathered), 'y', 0, 0)]
    dot_general x2 -> x0, matrix products: 2.74 us -> none  [the longest x1 2.22 us: per_device(): jnp.einsum('td,kde->kte', normed, w_kv, preferred_element_type=jnp.float32)]
    ppermute x1, waiting for transfers between devices: 0.93 us -> 3.01 us  [per_device(): after = lax.ppermute(latents[:1], line, [(j, i) for i, j in up])]
    pallas_call x1 -> x7, Pallas kernels: 18.4 us -> 16.3 us  [the longest x1 12.6 us: attend(): pl.pallas_call(attend_kernel, in_specs=[pl.BlockSpec(memory_space=pltpu.S...]
    slice x3 -> x1, local copies, waits for them, and re-layouts: 2.53 us -> 0.72 us  [per_device(): after = lax.ppermute(latents[:1], line, [(j, i) for i, j in up])]
  transfers between devices with their start and end apart: 12 -> 11, of which waited for: 6 -> 4; matrix products, arithmetic and copies ran while one was open for 3% -> 1% of each run, Pallas kernels for 0% -> 2%
where the time goes in v2:
time: 125 us; the launch traced here: 124 us
  starting transfers between devices  49.9 us (40%)
  blocking collectives  37.2 us (30%)
  Pallas kernels  17.4 us (14%)
  waiting for transfers between devices  11.7 us (9%)
  local copies, waits for them, and re-layouts  5.66 us (5%)
  between operations  1.51 us (1%)
    ppermute x4, starting transfers between devices, swap(): return lax.ppermute(value, 'zh', pairs)  19 us
    ppermute x3, starting transfers between devices, flip(): return lax.ppermute(value, PLANE, [(i, i ^ bits) for i in range(PEERS)])  18.1 us
    all_to_all x1, blocking collectives, per_device(): partial = lax.all_to_all(partial, PLANE, 0, 0)  15.6 us
    all_to_all x1, blocking collectives, per_device(): terms = lax.all_to_all(terms, 'head', 0, 0)  12.6 us
    pallas_call x1, Pallas kernels, attend(): pl.pallas_call(attend_kernel, in_specs=[pl.BlockSpec(memory_space=pltpu.S...  12.6 us
    all_gather x1, blocking collectives, per_device(): gathered = lax.all_gather(stem, 'head', axis=1, tiled=True)  8.96 us
    ppermute x4, waiting for transfers between devices, swap(): return lax.ppermute(value, 'zh', pairs)  5.05 us
    unnamed x24, local copies, waits for them, and re-layouts  4.89 us
  transfers between devices with their start and end apart: 11, of which 4 were waited for; matrix products, arithmetic and copies ran while one was open for 1% of the time, Pallas kernels for 2%

profile of v2, /device:TPU:1, one launch (start us, length us, event | category | flops | bytes accessed | tf_op | source)
XLA Modules:
  0.0 124.1 jit_solution(9081275479844656932)
XLA Ops:
  0.6 5.7 %collective-permute-start.5 = (bf16[1,2,128,128]{3,2,1,0:T(8,128)(2,1)}, bf16[1,2,128,128]{3,2,1,0:T(8,128)(2,1)S(1)}, u32[]{:S(2)}, u32[]{:S(2)}) collective-permute-start(bf16[1,2,128,128]{3,2,1,0:T(8,128)(2,1)} %bitcast.14), channel_id=1, source_target_pairs={{0,8},{8,0},{16,24},{24,16},{32,40},{40,32},{48,56},{56,48},{1,9},... | collective-permute-start | bytes 196616 | tf_op jit(solution)/shard_map/ppermute | solution.py:39
  6.4 0.7 fusion.7
  7.1 3.5 %collective-permute-start = (bf16[1,384]{1,0:T(2,128)(2,1)S(1)}, bf16[1,384]{1,0:T(2,128)(2,1)S(1)}, u32[]{:S(2)}, u32[]{:S(2)}) collective-permute-start(bf16[1,384]{1,0:T(2,128)(2,1)S(1)} %get-tuple-element.7), channel_id=1, source_target_pairs={{0,4},{4,8},{8,12},{12,16},{16,20},{20,24},{24,28},{28,32},{32,36}... | collective-permute-start | bytes 2312 | tf_op jit(solution)/shard_map/ppermute | solution.py:227
  10.6 1.3 %collective-permute-start.1 = (bf16[1,384]{1,0:T(2,128)(2,1)S(1)}, bf16[1,384]{1,0:T(2,128)(2,1)S(1)}, u32[]{:S(2)}, u32[]{:S(2)}) collective-permute-start(bf16[1,384]{1,0:T(2,128)(2,1)S(1)} %get-tuple-element.6), channel_id=1, source_target_pairs={{4,0},{8,4},{12,8},{16,12},{20,16},{24,20},{28,24},{32,28},{36,32}... | collective-permute-start | bytes 2312 | tf_op jit(solution)/shard_map/ppermute | solution.py:228
  11.9 3.0 %collective-permute-done.1.after_ref = bf16[1,384]{1,0:T(2,128)(2,1)S(1)} collective-permute-done((bf16[1,384]{1,0:T(2,128)(2,1)S(1)}, bf16[1,384]{1,0:T(2,128)(2,1)S(1)}, u32[]{:S(2)}, u32[]{:S(2)}) %collective-permute-start.1) | collective-permute-done | bytes 800 | tf_op jit(solution)/shard_map/ppermute | solution.py:228
  14.9 0.9 copy-done.7
  15.8 0.7 copy-done.8
  16.5 0.1 shard_map.104.refs_2_
  16.6 0.8 copy-done.3
  17.5 8.9 %collective-permute-start.6 = (bf16[2,2,128,128]{3,2,1,0:T(8,128)(2,1)S(1)}, bf16[2,2,128,128]{3,2,1,0:T(8,128)(2,1)S(1)}, u32[]{:S(2)}, u32[]{:S(2)}) collective-permute-start(bf16[2,2,128,128]{3,2,1,0:T(8,128)(2,1)S(1)} %bitcast.18), channel_id=1, source_target_pairs={{8,16},{16,8},{24,32},{32,24},{40,48},{48,40},{56,0},{0,56},{9,17}... | collective-permute-start | bytes 393224 | tf_op jit(solution)/shard_map/ppermute | solution.py:39
  26.3 9.0 %all_gather.3.x_ref.refs_3_ = bf16[128,1536]{1,0:T(8,128)(2,1)S(1)} all-gather(bf16[128,384]{1,0:T(8,128)(2,1)S(1)} %shard_map.104.refs_2_), channel_id=1, replica_groups=mesh['xh'=2,'y'=4,'zh'=8,'zl'=2,'head'=4] {'head'}, dimensions={1}, use_global_device_ids=true | all-gather | bytes 491520 | tf_op jit(solution)/shard_map/all_gather | solution.py:233
  35.3 1.1 shard_map.107
  36.4 0.7 copy-done.6
  37.1 4.2 %all-to-all-start = ((bf16[4,4,2,128,128]{4,3,2,1,0:T(8,128)(2,1)}), bf16[4,4,2,128,128]{4,3,2,1,0:T(8,128)(2,1)S(1)}, u32[]{:S(2)}, u32[]{:S(2)}) async-start(bf16[4,4,2,128,128]{4,3,2,1,0:T(8,128)(2,1)} %shard_map.107), calls=%async_computation | async-start | bytes 2097152 | tf_op jit(solution)/shard_map/all_to_all | solution.py:235
  41.9 2.2 %collective-permute-start.7 = (bf16[2,2,128,128]{3,2,1,0:T(8,128)(2,1)}, bf16[2,2,128,128]{3,2,1,0:T(8,128)(2,1)S(1)}, u32[]{:S(2)}, u32[]{:S(2)}) collective-permute-start(bf16[2,2,128,128]{3,2,1,0:T(8,128)(2,1)} %copy-done.6), channel_id=1, source_target_pairs={{0,8},{8,0},{16,24},{24,16},{32,40},{40,32},{48,56},{56,48},{1,9},... | collective-permute-start | bytes 393224 | tf_op jit(solution)/shard_map/ppermute | solution.py:39
  44.2 1.1 copy-done.2
  45.4 1.4 %shard_map.105 = (bf16[128,640]{1,0:T(8,128)(2,1)S(1)}, bf16[2,128,128]{2,1,0:T(8,128)(2,1)}) custom-call(bf16[128,1536]{1,0:T(8,128)(2,1)S(1)} %all_gather.3.x_ref.refs_3_, f32[1,1536]{1,0:T(1,128)S(1)} %broadcast_in_dim.6.mod_ref, bf16[1536,640]{1,0:T(8,128)(2,1)S(1)} %copy-done, bf16[2,1536,128]{2,1,0:T(8,128)(2,1)S(1)} %copy-done.2), custom_call_target="tpu_custom_call" | custom-call | flops 400000000 | bytes 5000000 | tf_op jit(solution)/shard_map/pallas_call | solution.py:184
  46.8 7.1 %collective-permute-start.2 = (bf16[128,640]{1,0:T(8,128)(2,1)S(1)}, bf16[128,640]{1,0:T(8,128)(2,1)S(1)}, u32[]{:S(2)}, u32[]{:S(2)}) collective-permute-start(bf16[128,640]{1,0:T(8,128)(2,1)S(1)} %get-tuple-element.4.refs_1_.refs_0_), channel_id=1, source_target_pairs={{0,4},{4,0},{256,260},{260,256},{1,5},{5,1},{257,261},{261,257},{2... | collective-permute-start | bytes 491528 | tf_op jit(solution)/shard_map/ppermute | solution.py:43
  53.9 0.7 copy-done.4
  54.5 2.3 %collective-permute-start.8 = (bf16[2,2,128,128]{3,2,1,0:T(8,128)(2,1)S(1)}, bf16[2,2,128,128]{3,2,1,0:T(8,128)(2,1)S(1)}, u32[]{:S(2)}, u32[]{:S(2)}) collective-permute-start(bf16[2,2,128,128]{3,2,1,0:T(8,128)(2,1)S(1)} %bitcast.17), channel_id=1, source_target_pairs={{8,16},{16,8},{24,32},{32,24},{40,48},{48,40},{56,0},{0,56},{9,17}... | collective-permute-start | bytes 393224 | tf_op jit(solution)/shard_map/ppermute | solution.py:39
  56.8 1.2 collective-permute-done.2.refs_2_.refs_1_
  58.0 5.0 %collective-permute-done.8.refs_1_ = bf16[2,2,128,128]{3,2,1,0:T(8,128)(2,1)S(1)} collective-permute-done((bf16[2,2,128,128]{3,2,1,0:T(8,128)(2,1)S(1)}, bf16[2,2,128,128]{3,2,1,0:T(8,128)(2,1)S(1)}, u32[]{:S(2)}, u32[]{:S(2)}) %collective-permute-start.8) | collective-permute-done | bytes 131104 | tf_op jit(solution)/shard_map/ppermute | solution.py:39
  63.1 1.1 shard_map.109
  64.2 3.8 %all-to-all-start.1 = ((bf16[4,4,2,128,128]{4,3,2,1,0:T(8,128)(2,1)}), bf16[4,4,2,128,128]{4,3,2,1,0:T(8,128)(2,1)S(1)}, u32[]{:S(2)}, u32[]{:S(2)}) async-start(bf16[4,4,2,128,128]{4,3,2,1,0:T(8,128)(2,1)} %shard_map.109), calls=%async_computation.1 | async-start | bytes 2097152 | tf_op jit(solution)/shard_map/all_to_all | solution.py:240
  67.9 2.2 %collective-permute-start.3 = (bf16[128,640]{1,0:T(8,128)(2,1)S(1)}, bf16[128,640]{1,0:T(8,128)(2,1)S(1)}, u32[]{:S(2)}, u32[]{:S(2)}) collective-permute-start(bf16[128,640]{1,0:T(8,128)(2,1)S(1)} %copy-done.5), channel_id=1, source_target_pairs={{0,256},{4,260},{256,0},{260,4},{1,257},{5,261},{257,1},{261,5},{2... | collective-permute-start | bytes 491528 | tf_op jit(solution)/shard_map/ppermute | solution.py:43
  70.1 8.9 %collective-permute-start.4 = (bf16[128,640]{1,0:T(8,128)(2,1)S(1)}, bf16[128,640]{1,0:T(8,128)(2,1)S(1)}, u32[]{:S(2)}, u32[]{:S(2)}) collective-permute-start(bf16[128,640]{1,0:T(8,128)(2,1)S(1)} %copy-done.5), channel_id=1, source_target_pairs={{0,260},{4,256},{256,4},{260,0},{1,261},{5,257},{257,5},{261,1},{2... | collective-permute-start | bytes 491528 | tf_op jit(solution)/shard_map/ppermute | solution.py:43
  79.1 2.4 %collective-permute-done.4.refs_3_ = bf16[128,640]{1,0:T(8,128)(2,1)S(1)} collective-permute-done((bf16[128,640]{1,0:T(8,128)(2,1)S(1)}, bf16[128,640]{1,0:T(8,128)(2,1)S(1)}, u32[]{:S(2)}, u32[]{:S(2)}) %collective-permute-start.4) | collective-permute-done | bytes 163872 | tf_op jit(solution)/shard_map/ppermute | solution.py:43
  81.5 12.6 %shard_map.110 = bf16[4,128,768]{2,1,0:T(8,128)(2,1)S(1)} custom-call(s32[2]{0:T(128)S(1)} %pad_add_fusion.where_ref, bf16[128,640]{1,0:T(8,128)(2,1)S(1)} %copy-done.5, bf16[128,640]{1,0:T(8,128)(2,1)S(1)} %collective-permute-done.2.refs_2_.refs_1_, bf16[128,640]{1,0:T(8,128)(2,1)S(1)} %collective-permute-done.3.refs_2_, ...), custom_call_target="tpu_custom_call" | custom-call | flops 15000000512 | bytes 4000000 | tf_op jit(solution)/shard_map/pallas_call | solution.py:112
  94.1 15.6 %all_to_all.20.parts_ref = bf16[4,128,768]{2,1,0:T(8,128)(2,1)S(1)} all-to-all(bf16[4,128,768]{2,1,0:T(8,128)(2,1)S(1)} %shard_map.110), channel_id=1, replica_groups=mesh['xh'=2,'y'=4,'zh'=8,'zl'=2,'head'=4] {'xh','zl'}, dimensions={0} | all-to-all | bytes 1572864 | tf_op jit(solution)/shard_map/all_to_all | solution.py:243
  109.7 1.1 shard_map.111
  110.8 12.6 %all_to_all.21 = bf16[4,128,384]{2,1,0:T(8,128)(2,1)S(1)} all-to-all(bf16[4,128,384]{2,1,0:T(8,128)(2,1)S(1)} %bitcast.19), channel_id=1, replica_groups=mesh['xh'=2,'y'=4,'zh'=8,'zl'=2,'head'=4] {'head'}, dimensions={0} | all-to-all | bytes 786432 | tf_op jit(solution)/shard_map/all_to_all | solution.py:246
  123.5 0.7 add_convert_fusion
  (32 shorter events, 0.3 us)
Async XLA Ops:
  0.6 16.0 %collective-permute-start.5 = (bf16[1,2,128,128]{3,2,1,0:T(8,128)(2,1)}, bf16[1,2,128,128]{3,2,1,0:T(8,128)(2,1)S(1)}, u32[]{:S(2)}, u32[]{:S(2)}) collective-permute-start(bf16[1,2,128,128]{3,2,1,0:T(8,128)(2,1)} %bitcast.14), channel_id=1, source_target_pairs={{0,8},{8,0},{16,24},{24,16},{32,40},{40,32},{48,56},{56,48},{1,9},... | collective-permute-start | bytes 196616 | tf_op jit(solution)/shard_map/ppermute | solution.py:39
  7.1 4.8 %collective-permute-start = (bf16[1,384]{1,0:T(2,128)(2,1)S(1)}, bf16[1,384]{1,0:T(2,128)(2,1)S(1)}, u32[]{:S(2)}, u32[]{:S(2)}) collective-permute-start(bf16[1,384]{1,0:T(2,128)(2,1)S(1)} %get-tuple-element.7), channel_id=1, source_target_pairs={{0,4},{4,8},{8,12},{12,16},{16,20},{20,24},{24,28},{28,32},{32,36}... | collective-permute-start | bytes 2312 | tf_op jit(solution)/shard_map/ppermute | solution.py:227
  10.6 4.3 %collective-permute-start.1 = (bf16[1,384]{1,0:T(2,128)(2,1)S(1)}, bf16[1,384]{1,0:T(2,128)(2,1)S(1)}, u32[]{:S(2)}, u32[]{:S(2)}) collective-permute-start(bf16[1,384]{1,0:T(2,128)(2,1)S(1)} %get-tuple-element.6), channel_id=1, source_target_pairs={{4,0},{8,4},{12,8},{16,12},{20,16},{24,20},{28,24},{32,28},{36,32}... | collective-permute-start | bytes 2312 | tf_op jit(solution)/shard_map/ppermute | solution.py:228
  14.9 0.9 copy-start.7
  15.8 0.7 copy-start.8
  16.6 0.8 copy-start.3
  17.5 17.8 %collective-permute-start.6 = (bf16[2,2,128,128]{3,2,1,0:T(8,128)(2,1)S(1)}, bf16[2,2,128,128]{3,2,1,0:T(8,128)(2,1)S(1)}, u32[]{:S(2)}, u32[]{:S(2)}) collective-permute-start(bf16[2,2,128,128]{3,2,1,0:T(8,128)(2,1)S(1)} %bitcast.18), channel_id=1, source_target_pairs={{8,16},{16,8},{24,32},{32,24},{40,48},{48,40},{56,0},{0,56},{9,17}... | collective-permute-start | bytes 393224 | tf_op jit(solution)/shard_map/ppermute | solution.py:39
  35.3 8.8 %copy-start.10 = (f32[1536]{0:T(1024)S(1)}, f32[1536]{0:T(1024)}, u32[]{:S(2)}) copy-start(f32[1536]{0:T(1024)} %param.12) | copy-start | bytes 18436
  35.3 8.8 %copy-start.11 = (f32[1536]{0:T(1024)S(1)}, f32[1536]{0:T(1024)}, u32[]{:S(2)}) copy-start(f32[1536]{0:T(1024)} %param.13) | copy-start | bytes 18436
  35.3 8.9 %copy-start = (bf16[1536,640]{1,0:T(8,128)(2,1)S(1)}, bf16[1536,640]{1,0:T(8,128)(2,1)}, u32[]{:S(2)}) copy-start(bf16[1536,640]{1,0:T(8,128)(2,1)} %wq_ref.1) | copy-start | bytes 5898244
  36.4 0.7 copy-start.6
  37.1 27.1 %all-to-all-start = ((bf16[4,4,2,128,128]{4,3,2,1,0:T(8,128)(2,1)}), bf16[4,4,2,128,128]{4,3,2,1,0:T(8,128)(2,1)S(1)}, u32[]{:S(2)}, u32[]{:S(2)}) async-start(bf16[4,4,2,128,128]{4,3,2,1,0:T(8,128)(2,1)} %shard_map.107), calls=%async_computation | async-start | bytes 2097152 | tf_op jit(solution)/shard_map/all_to_all | solution.py:235
  41.9 11.9 %collective-permute-start.7 = (bf16[2,2,128,128]{3,2,1,0:T(8,128)(2,1)}, bf16[2,2,128,128]{3,2,1,0:T(8,128)(2,1)S(1)}, u32[]{:S(2)}, u32[]{:S(2)}) collective-permute-start(bf16[2,2,128,128]{3,2,1,0:T(8,128)(2,1)} %copy-done.6), channel_id=1, source_target_pairs={{0,8},{8,0},{16,24},{24,16},{32,40},{40,32},{48,56},{56,48},{1,9},... | collective-permute-start | bytes 393224 | tf_op jit(solution)/shard_map/ppermute | solution.py:39
  44.2 1.1 copy-start.2
  46.8 34.7 %copy-start.9 = (bf16[2,128,128]{2,1,0:T(8,128)(2,1)S(1)}, bf16[2,128,128]{2,1,0:T(8,128)(2,1)}, u32[]{:S(2)}) copy-start(bf16[2,128,128]{2,1,0:T(8,128)(2,1)} %get-tuple-element.3.refs_6_) | copy-start | bytes 196612
  46.8 11.2 %collective-permute-start.2 = (bf16[128,640]{1,0:T(8,128)(2,1)S(1)}, bf16[128,640]{1,0:T(8,128)(2,1)S(1)}, u32[]{:S(2)}, u32[]{:S(2)}) collective-permute-start(bf16[128,640]{1,0:T(8,128)(2,1)S(1)} %get-tuple-element.4.refs_1_.refs_0_), channel_id=1, source_target_pairs={{0,4},{4,0},{256,260},{260,256},{1,5},{5,1},{257,261},{261,257},{2... | collective-permute-start | bytes 491528 | tf_op jit(solution)/shard_map/ppermute | solution.py:43
  53.9 0.7 copy-start.4
  54.5 13.4 %copy-start.5 = (bf16[128,640]{1,0:T(8,128)(2,1)S(1)}, bf16[128,640]{1,0:T(8,128)(2,1)}, u32[]{:S(2)}) copy-start(bf16[128,640]{1,0:T(8,128)(2,1)} %copy-done.4) | copy-start | bytes 491524
  54.5 8.5 %collective-permute-start.8 = (bf16[2,2,128,128]{3,2,1,0:T(8,128)(2,1)S(1)}, bf16[2,2,128,128]{3,2,1,0:T(8,128)(2,1)S(1)}, u32[]{:S(2)}, u32[]{:S(2)}) collective-permute-start(bf16[2,2,128,128]{3,2,1,0:T(8,128)(2,1)S(1)} %bitcast.17), channel_id=1, source_target_pairs={{8,16},{16,8},{24,32},{32,24},{40,48},{48,40},{56,0},{0,56},{9,17}... | collective-permute-start | bytes 393224 | tf_op jit(solution)/shard_map/ppermute | solution.py:39
  64.2 17.4 %all-to-all-start.1 = ((bf16[4,4,2,128,128]{4,3,2,1,0:T(8,128)(2,1)}), bf16[4,4,2,128,128]{4,3,2,1,0:T(8,128)(2,1)S(1)}, u32[]{:S(2)}, u32[]{:S(2)}) async-start(bf16[4,4,2,128,128]{4,3,2,1,0:T(8,128)(2,1)} %shard_map.109), calls=%async_computation.1 | async-start | bytes 2097152 | tf_op jit(solution)/shard_map/all_to_all | solution.py:240
  67.9 11.2 %collective-permute-start.3 = (bf16[128,640]{1,0:T(8,128)(2,1)S(1)}, bf16[128,640]{1,0:T(8,128)(2,1)S(1)}, u32[]{:S(2)}, u32[]{:S(2)}) collective-permute-start(bf16[128,640]{1,0:T(8,128)(2,1)S(1)} %copy-done.5), channel_id=1, source_target_pairs={{0,256},{4,260},{256,0},{260,4},{1,257},{5,261},{257,1},{261,5},{2... | collective-permute-start | bytes 491528 | tf_op jit(solution)/shard_map/ppermute | solution.py:43
  70.1 11.4 %collective-permute-start.4 = (bf16[128,640]{1,0:T(8,128)(2,1)S(1)}, bf16[128,640]{1,0:T(8,128)(2,1)S(1)}, u32[]{:S(2)}, u32[]{:S(2)}) collective-permute-start(bf16[128,640]{1,0:T(8,128)(2,1)S(1)} %copy-done.5), channel_id=1, source_target_pairs={{0,260},{4,256},{256,4},{260,0},{1,261},{5,257},{257,5},{261,1},{2... | collective-permute-start | bytes 491528 | tf_op jit(solution)/shard_map/ppermute | solution.py:43
  81.5 28.2 %copy-start.1 = (bf16[640,1536]{1,0:T(8,128)(2,1)S(1)}, bf16[640,1536]{1,0:T(8,128)(2,1)}, u32[]{:S(2)}) copy-start(bf16[640,1536]{1,0:T(8,128)(2,1)} %w_ref.3) | copy-start | bytes 5898244

commit v3 on v2

--- a/solution.py
+++ b/solution.py
@@ -136,17 +136,17 @@
             row += n
 
 
-def spread(parts, n, behind):
+def spread(parts, n, *behind):
     blocks = sum(p.shape[0] for p in parts)
     vmem = pl.BlockSpec(memory_space=pltpu.VMEM)
     return pl.pallas_call(
         functools.partial(copies_kernel, len(parts)),
-        in_specs=[vmem] * len(parts) + [pl.BlockSpec(memory_space=pl.ANY)],
+        in_specs=[vmem] * len(parts) + [pl.BlockSpec(memory_space=pl.ANY)] * len(behind),
         out_specs=vmem,
         out_shape=jax.ShapeDtypeStruct((n, blocks) + parts[0].shape[1:], jnp.bfloat16),
         compiler_params=pltpu.CompilerParams(vmem_limit_bytes=VMEM_LIMIT),
         cost_estimate=pl.CostEstimate(flops=10**5, bytes_accessed=10**6, transcendentals=0),
-    )(*parts, behind)
+    )(*parts, *behind)
 
 
 def stem_kernel(x_ref, before_ref, after_ref, w_ref, stem_ref):
@@ -232,13 +232,12 @@
     got.append(swap(spread([own] + got, 1, stem)[0], 1))
     gathered = lax.all_gather(stem, "head", axis=1, tiled=True)
     modulate = norm_gain * (1.0 + 0.3 * ada_gain * embed(timestep, gathered.shape[1]))
+    got.append(swap(got[1], 0))
     near = lax.all_to_all(spread([own] + got, 4, gathered), "y", 0, 0)
-    got.append(swap(got[1], 0))
     queries, fresh = project(gathered, modulate[None], w_query, w_kv)
-    got.append(swap(spread(got[2:3], 1, queries)[0], 1))
     all_queries = [queries] + [flip(queries, bits) for bits in range(1, PEERS)]
-    far = lax.all_to_all(spread(got[2:], 4, all_queries[1]), "y", 0, 0)
-    where = jnp.stack([lax.axis_index(PLANE), 4 * lax.axis_index("y")]).astype(jnp.int32)
+    far = lax.all_to_all(spread([swap(got[2], 1)], 4, all_queries[1], all_queries[2]), "y", 0, 0)
+    where = jnp.stack([lax.axis_index(PLANE), 6 * lax.axis_index("y")]).astype(jnp.int32)
     partial = attend(where, all_queries, near, far, fresh)
     partial = lax.all_to_all(partial, PLANE, 0, 0)
     terms = merge(partial, w_out)

time: 125 us -> 144 us (1.15)
  waiting for transfers between devices: 11.7 us -> 31.7 us
  starting transfers between devices: 49.9 us -> 47.5 us
    all_to_all x1, waiting for transfers between devices: 0.01 us -> 10.6 us  [per_device(): near = lax.all_to_all(spread([own] + got, 4, gathered), 'y', 0, 0)]
    all_to_all x1, waiting for transfers between devices: 0.01 us -> 7.39 us  [per_device(): lax.all_to_all(spread([swap(got[2], 1)], 4, all_queries[1], all_queries[2...]
    ppermute x3, starting transfers between devices: 18.1 us -> 12.6 us  [flip(): return lax.ppermute(value, PLANE, [(i, i ^ bits) for i in range(PEERS)])]
    ppermute x4, starting transfers between devices: 19 us -> 22.3 us  [swap(): return lax.ppermute(value, 'zh', pairs)]
    all_to_all x1, blocking collectives: 15.6 us -> 13.3 us  [per_device(): partial = lax.all_to_all(partial, PLANE, 0, 0)]
    ppermute x4, waiting for transfers between devices: 5.05 us -> 7.31 us  [swap(): return lax.ppermute(value, 'zh', pairs)]
    all_gather x1, blocking collectives: 8.96 us -> 11 us  [per_device(): gathered = lax.all_gather(stem, 'head', axis=1, tiled=True)]
    unnamed x24 -> x16, local copies, waits for them, and re-layouts: 4.89 us -> 5.11 us
  transfers between devices with their start and end apart: 11 -> 11, of which waited for: 4 -> 6; matrix products, arithmetic and copies ran while one was open for 1% -> 1% of each run, Pallas kernels for 2% -> 2%
where the time goes in v3:
time: 144 us; the launch traced here: 143 us
  starting transfers between devices  47.5 us (33%)
  blocking collectives  37.5 us (26%)
  waiting for transfers between devices  31.7 us (22%)
  Pallas kernels  17.4 us (12%)
  local copies, waits for them, and re-layouts  5.87 us (4%)
  other arithmetic  1.57 us (1%)
  between operations  1.47 us (1%)
    ppermute x4, starting transfers between devices, swap(): return lax.ppermute(value, 'zh', pairs)  22.3 us
    all_to_all x1, blocking collectives, per_device(): partial = lax.all_to_all(partial, PLANE, 0, 0)  13.3 us
    all_to_all x1, blocking collectives, per_device(): terms = lax.all_to_all(terms, 'head', 0, 0)  13.2 us
    ppermute x3, starting transfers between devices, flip(): return lax.ppermute(value, PLANE, [(i, i ^ bits) for i in range(PEERS)])  12.6 us
    pallas_call x1, Pallas kernels, attend(): pl.pallas_call(attend_kernel, in_specs=[pl.BlockSpec(memory_space=pltpu.S...  12.6 us
    all_gather x1, blocking collectives, per_device(): gathered = lax.all_gather(stem, 'head', axis=1, tiled=True)  11 us
    all_to_all x1, waiting for transfers between devices, per_device(): near = lax.all_to_all(spread([own] + got, 4, gathered), 'y', 0, 0)  10.6 us
    all_to_all x1, waiting for transfers between devices, per_device(): lax.all_to_all(spread([swap(got[2], 1)], 4, all_queries[1], all_queries[2...  7.39 us
  transfers between devices with their start and end apart: 11, of which 6 were waited for; matrix products, arithmetic and copies ran while one was open for 1% of the time, Pallas kernels for 2%

profile of v3, /device:TPU:1, one launch (start us, length us, event | category | flops | bytes accessed | tf_op | source)
XLA Modules:
  0.0 143.0 jit_solution(14844763783514625807)
XLA Ops:
  0.6 5.7 %collective-permute-start.5 = (bf16[1,2,128,128]{3,2,1,0:T(8,128)(2,1)}, bf16[1,2,128,128]{3,2,1,0:T(8,128)(2,1)S(1)}, u32[]{:S(2)}, u32[]{:S(2)}) collective-permute-start(bf16[1,2,128,128]{3,2,1,0:T(8,128)(2,1)} %bitcast.13), channel_id=1, source_target_pairs={{0,8},{8,0},{16,24},{24,16},{32,40},{40,32},{48,56},{56,48},{1,9},... | collective-permute-start | bytes 196616 | tf_op jit(solution)/shard_map/ppermute | solution.py:39
  6.4 0.7 fusion.7
  7.1 3.5 %collective-permute-start = (bf16[1,384]{1,0:T(2,128)(2,1)S(1)}, bf16[1,384]{1,0:T(2,128)(2,1)S(1)}, u32[]{:S(2)}, u32[]{:S(2)}) collective-permute-start(bf16[1,384]{1,0:T(2,128)(2,1)S(1)} %get-tuple-element.7), channel_id=1, source_target_pairs={{0,4},{4,8},{8,12},{12,16},{16,20},{20,24},{24,28},{28,32},{32,36}... | collective-permute-start | bytes 2312 | tf_op jit(solution)/shard_map/ppermute | solution.py:227
  10.6 1.3 collective-permute-start.1
  12.6 2.4 %collective-permute-done.1.after_ref = bf16[1,384]{1,0:T(2,128)(2,1)S(1)} collective-permute-done((bf16[1,384]{1,0:T(2,128)(2,1)S(1)}, bf16[1,384]{1,0:T(2,128)(2,1)S(1)}, u32[]{:S(2)}, u32[]{:S(2)}) %collective-permute-start.1) | collective-permute-done | bytes 800 | tf_op jit(solution)/shard_map/ppermute | solution.py:228
  14.9 0.9 copy-done.5
  15.8 0.7 copy-done.6
  16.6 0.8 copy-done.3
  17.5 8.9 %collective-permute-start.6 = (bf16[2,2,128,128]{3,2,1,0:T(8,128)(2,1)S(1)}, bf16[2,2,128,128]{3,2,1,0:T(8,128)(2,1)S(1)}, u32[]{:S(2)}, u32[]{:S(2)}) collective-permute-start(bf16[2,2,128,128]{3,2,1,0:T(8,128)(2,1)S(1)} %bitcast.16), channel_id=1, source_target_pairs={{8,16},{16,8},{24,32},{32,24},{40,48},{48,40},{56,0},{0,56},{9,17}... | collective-permute-start | bytes 393224 | tf_op jit(solution)/shard_map/ppermute | solution.py:39
  26.3 0.8 add_multiply_fusion
  27.1 1.6 %collective-permute-done.6.refs_2_ = bf16[2,2,128,128]{3,2,1,0:T(8,128)(2,1)S(1)} collective-permute-done((bf16[2,2,128,128]{3,2,1,0:T(8,128)(2,1)S(1)}, bf16[2,2,128,128]{3,2,1,0:T(8,128)(2,1)S(1)}, u32[]{:S(2)}, u32[]{:S(2)}) %collective-permute-start.6) | collective-permute-done | bytes 131104 | tf_op jit(solution)/shard_map/ppermute | solution.py:39
  28.7 2.9 %collective-permute-start.7 = (bf16[2,2,128,128]{3,2,1,0:T(8,128)(2,1)S(1)}, bf16[2,2,128,128]{3,2,1,0:T(8,128)(2,1)S(1)}, u32[]{:S(2)}, u32[]{:S(2)}) collective-permute-start(bf16[2,2,128,128]{3,2,1,0:T(8,128)(2,1)S(1)} %collective-permute-done.6.refs_2_), channel_id=1, source_target_pairs={{0,8},{8,0},{16,24},{24,16},{32,40},{40,32},{48,56},{56,48},{1,9},... | collective-permute-start | bytes 393224 | tf_op jit(solution)/shard_map/ppermute | solution.py:39
  31.6 11.0 %all_gather.3.x_ref.refs_4_ = bf16[128,1536]{1,0:T(8,128)(2,1)S(1)} all-gather(bf16[128,384]{1,0:T(8,128)(2,1)S(1)} %shard_map.104.refs_2_), channel_id=1, replica_groups=mesh['xh'=2,'y'=4,'zh'=8,'zl'=2,'head'=4] {'head'}, dimensions={1}, use_global_device_ids=true | all-gather | bytes 491520 | tf_op jit(solution)/shard_map/all_gather | solution.py:233
  42.7 1.5 %copy-done = bf16[1536,640]{1,0:T(8,128)(2,1)S(1)} copy-done((bf16[1536,640]{1,0:T(8,128)(2,1)S(1)}, bf16[1536,640]{1,0:T(8,128)(2,1)}, u32[]{:S(2)}) %copy-start) | copy-done | bytes 1966104
  44.2 1.1 copy-done.2
  45.3 1.4 %shard_map.105 = (bf16[128,640]{1,0:T(8,128)(2,1)S(1)}, bf16[2,128,128]{2,1,0:T(8,128)(2,1)}) custom-call(bf16[128,1536]{1,0:T(8,128)(2,1)S(1)} %all_gather.3.x_ref.refs_4_, f32[1,1536]{1,0:T(1,128)S(1)} %broadcast_in_dim.6.mod_ref, bf16[1536,640]{1,0:T(8,128)(2,1)S(1)} %copy-done, bf16[2,1536,128]{2,1,0:T(8,128)(2,1)S(1)} %copy-done.2), custom_call_target="tpu_custom_call" | custom-call | flops 400000000 | bytes 5000000 | tf_op jit(solution)/shard_map/pallas_call | solution.py:184
  46.8 3.6 %collective-permute-start.2 = (bf16[128,640]{1,0:T(8,128)(2,1)S(1)}, bf16[128,640]{1,0:T(8,128)(2,1)S(1)}, u32[]{:S(2)}, u32[]{:S(2)}) collective-permute-start(bf16[128,640]{1,0:T(8,128)(2,1)S(1)} %get-tuple-element.4.refs_0_), channel_id=1, source_target_pairs={{0,4},{4,0},{256,260},{260,256},{1,5},{5,1},{257,261},{261,257},{2... | collective-permute-start | bytes 491528 | tf_op jit(solution)/shard_map/ppermute | solution.py:43
  50.4 4.6 %collective-permute-start.3 = (bf16[128,640]{1,0:T(8,128)(2,1)S(1)}, bf16[128,640]{1,0:T(8,128)(2,1)S(1)}, u32[]{:S(2)}, u32[]{:S(2)}) collective-permute-start(bf16[128,640]{1,0:T(8,128)(2,1)S(1)} %get-tuple-element.4.refs_0_), channel_id=1, source_target_pairs={{0,256},{4,260},{256,0},{260,4},{1,257},{5,261},{257,1},{261,5},{2... | collective-permute-start | bytes 491528 | tf_op jit(solution)/shard_map/ppermute | solution.py:43
  55.1 4.9 %collective-permute-start.8 = (bf16[2,2,128,128]{3,2,1,0:T(8,128)(2,1)S(1)}, bf16[2,2,128,128]{3,2,1,0:T(8,128)(2,1)S(1)}, u32[]{:S(2)}, u32[]{:S(2)}) collective-permute-start(bf16[2,2,128,128]{3,2,1,0:T(8,128)(2,1)S(1)} %collective-permute-done.7.refs_3_), channel_id=1, source_target_pairs={{8,16},{16,8},{24,32},{32,24},{40,48},{48,40},{56,0},{0,56},{9,17}... | collective-permute-start | bytes 393224 | tf_op jit(solution)/shard_map/ppermute | solution.py:39
  59.9 5.7 %collective-permute-done.8.refs_0_ = bf16[2,2,128,128]{3,2,1,0:T(8,128)(2,1)S(1)} collective-permute-done((bf16[2,2,128,128]{3,2,1,0:T(8,128)(2,1)S(1)}, bf16[2,2,128,128]{3,2,1,0:T(8,128)(2,1)S(1)}, u32[]{:S(2)}, u32[]{:S(2)}) %collective-permute-start.8) | collective-permute-done | bytes 131104 | tf_op jit(solution)/shard_map/ppermute | solution.py:39
  65.6 0.9 shard_map.108
  66.5 4.2 %all-to-all-start.1 = ((bf16[4,2,2,128,128]{4,3,2,1,0:T(8,128)(2,1)}), bf16[4,2,2,128,128]{4,3,2,1,0:T(8,128)(2,1)S(1)}, u32[]{:S(2)}, u32[]{:S(2)}) async-start(bf16[4,2,2,128,128]{4,3,2,1,0:T(8,128)(2,1)} %shard_map.108), calls=%async_computation.1 | async-start | bytes 1048576 | tf_op jit(solution)/shard_map/all_to_all | solution.py:239
  70.7 1.4 shard_map.107
  72.1 7.4 %all-to-all-done.1.refs_5_ = bf16[4,2,2,128,128]{4,3,2,1,0:T(8,128)(2,1)S(1)} async-done(((bf16[4,2,2,128,128]{4,3,2,1,0:T(8,128)(2,1)}), bf16[4,2,2,128,128]{4,3,2,1,0:T(8,128)(2,1)S(1)}, u32[]{:S(2)}, u32[]{:S(2)}) %all-to-all-start.1) | async-done | bytes 524320 | tf_op jit(solution)/shard_map/all_to_all | solution.py:239
  79.5 3.6 %all-to-all-start = ((bf16[4,6,2,128,128]{4,3,2,1,0:T(8,128)(2,1)}), bf16[4,6,2,128,128]{4,3,2,1,0:T(8,128)(2,1)S(1)}, u32[]{:S(2)}, u32[]{:S(2)}) async-start(bf16[4,6,2,128,128]{4,3,2,1,0:T(8,128)(2,1)} %shard_map.107), calls=%async_computation | async-start | bytes 3145728 | tf_op jit(solution)/shard_map/all_to_all | solution.py:236
  83.1 4.4 %collective-permute-start.4 = (bf16[128,640]{1,0:T(8,128)(2,1)S(1)}, bf16[128,640]{1,0:T(8,128)(2,1)S(1)}, u32[]{:S(2)}, u32[]{:S(2)}) collective-permute-start(bf16[128,640]{1,0:T(8,128)(2,1)S(1)} %get-tuple-element.4.refs_0_), channel_id=1, source_target_pairs={{0,260},{4,256},{256,4},{260,0},{1,261},{5,257},{257,5},{261,1},{2... | collective-permute-start | bytes 491528 | tf_op jit(solution)/shard_map/ppermute | solution.py:43
  87.5 4.0 %collective-permute-done.4.refs_3_ = bf16[128,640]{1,0:T(8,128)(2,1)S(1)} collective-permute-done((bf16[128,640]{1,0:T(8,128)(2,1)S(1)}, bf16[128,640]{1,0:T(8,128)(2,1)S(1)}, u32[]{:S(2)}, u32[]{:S(2)}) %collective-permute-start.4) | collective-permute-done | bytes 163872 | tf_op jit(solution)/shard_map/ppermute | solution.py:43
  91.5 10.6 %all-to-all-done.refs_4_ = bf16[4,6,2,128,128]{4,3,2,1,0:T(8,128)(2,1)S(1)} async-done(((bf16[4,6,2,128,128]{4,3,2,1,0:T(8,128)(2,1)}), bf16[4,6,2,128,128]{4,3,2,1,0:T(8,128)(2,1)S(1)}, u32[]{:S(2)}, u32[]{:S(2)}) %all-to-all-start) | async-done | bytes 1572896 | tf_op jit(solution)/shard_map/all_to_all | solution.py:236
  102.1 12.6 %shard_map.109 = bf16[4,128,768]{2,1,0:T(8,128)(2,1)S(1)} custom-call(s32[2]{0:T(128)S(1)} %pad_add_fusion.where_ref, bf16[128,640]{1,0:T(8,128)(2,1)S(1)} %get-tuple-element.4.refs_0_, bf16[128,640]{1,0:T(8,128)(2,1)S(1)} %collective-permute-done.2.refs_1_, bf16[128,640]{1,0:T(8,128)(2,1)S(1)} %collective-permute-done.3.refs_2_, ...), custom_call_target="tpu_custom_call" | custom-call | flops 15000000512 | bytes 4000000 | tf_op jit(solution)/shard_map/pallas_call | solution.py:112
  114.7 13.3 %all_to_all.20.parts_ref = bf16[4,128,768]{2,1,0:T(8,128)(2,1)S(1)} all-to-all(bf16[4,128,768]{2,1,0:T(8,128)(2,1)S(1)} %shard_map.109), channel_id=1, replica_groups=mesh['xh'=2,'y'=4,'zh'=8,'zl'=2,'head'=4] {'xh','zl'}, dimensions={0} | all-to-all | bytes 1572864 | tf_op jit(solution)/shard_map/all_to_all | solution.py:242
  128.0 1.1 shard_map.110
  129.1 13.2 %all_to_all.21 = bf16[4,128,384]{2,1,0:T(8,128)(2,1)S(1)} all-to-all(bf16[4,128,384]{2,1,0:T(8,128)(2,1)S(1)} %bitcast.17), channel_id=1, replica_groups=mesh['xh'=2,'y'=4,'zh'=8,'zl'=2,'head'=4] {'head'}, dimensions={0} | all-to-all | bytes 786432 | tf_op jit(solution)/shard_map/all_to_all | solution.py:245
  (23 shorter events, 1.0 us)
Async XLA Ops:
  0.6 16.0 %collective-permute-start.5 = (bf16[1,2,128,128]{3,2,1,0:T(8,128)(2,1)}, bf16[1,2,128,128]{3,2,1,0:T(8,128)(2,1)S(1)}, u32[]{:S(2)}, u32[]{:S(2)}) collective-permute-start(bf16[1,2,128,128]{3,2,1,0:T(8,128)(2,1)} %bitcast.13), channel_id=1, source_target_pairs={{0,8},{8,0},{16,24},{24,16},{32,40},{40,32},{48,56},{56,48},{1,9},... | collective-permute-start | bytes 196616 | tf_op jit(solution)/shard_map/ppermute | solution.py:39
  7.1 5.5 %collective-permute-start = (bf16[1,384]{1,0:T(2,128)(2,1)S(1)}, bf16[1,384]{1,0:T(2,128)(2,1)S(1)}, u32[]{:S(2)}, u32[]{:S(2)}) collective-permute-start(bf16[1,384]{1,0:T(2,128)(2,1)S(1)} %get-tuple-element.7), channel_id=1, source_target_pairs={{0,4},{4,8},{8,12},{12,16},{16,20},{20,24},{24,28},{28,32},{32,36}... | collective-permute-start | bytes 2312 | tf_op jit(solution)/shard_map/ppermute | solution.py:227
  10.6 4.3 %collective-permute-start.1 = (bf16[1,384]{1,0:T(2,128)(2,1)S(1)}, bf16[1,384]{1,0:T(2,128)(2,1)S(1)}, u32[]{:S(2)}, u32[]{:S(2)}) collective-permute-start(bf16[1,384]{1,0:T(2,128)(2,1)S(1)} %get-tuple-element.6), channel_id=1, source_target_pairs={{4,0},{8,4},{12,8},{16,12},{20,16},{24,20},{28,24},{32,28},{36,32}... | collective-permute-start | bytes 2312 | tf_op jit(solution)/shard_map/ppermute | solution.py:228
  14.9 0.9 copy-start.5
  15.8 0.7 copy-start.6
  16.6 0.8 copy-start.3
  17.5 11.3 %collective-permute-start.6 = (bf16[2,2,128,128]{3,2,1,0:T(8,128)(2,1)S(1)}, bf16[2,2,128,128]{3,2,1,0:T(8,128)(2,1)S(1)}, u32[]{:S(2)}, u32[]{:S(2)}) collective-permute-start(bf16[2,2,128,128]{3,2,1,0:T(8,128)(2,1)S(1)} %bitcast.16), channel_id=1, source_target_pairs={{8,16},{16,8},{24,32},{32,24},{40,48},{48,40},{56,0},{0,56},{9,17}... | collective-permute-start | bytes 393224 | tf_op jit(solution)/shard_map/ppermute | solution.py:39
  28.7 26.3 %collective-permute-start.7 = (bf16[2,2,128,128]{3,2,1,0:T(8,128)(2,1)S(1)}, bf16[2,2,128,128]{3,2,1,0:T(8,128)(2,1)S(1)}, u32[]{:S(2)}, u32[]{:S(2)}) collective-permute-start(bf16[2,2,128,128]{3,2,1,0:T(8,128)(2,1)S(1)} %collective-permute-done.6.refs_2_), channel_id=1, source_target_pairs={{0,8},{8,0},{16,24},{24,16},{32,40},{40,32},{48,56},{56,48},{1,9},... | collective-permute-start | bytes 393224 | tf_op jit(solution)/shard_map/ppermute | solution.py:39
  42.6 1.5 %copy-start = (bf16[1536,640]{1,0:T(8,128)(2,1)S(1)}, bf16[1536,640]{1,0:T(8,128)(2,1)}, u32[]{:S(2)}) copy-start(bf16[1536,640]{1,0:T(8,128)(2,1)} %wq_ref.1) | copy-start | bytes 5898244
  44.2 1.1 copy-start.2
  45.3 25.4 %copy-start.4 = (bf16[2,128,128]{2,1,0:T(8,128)(2,1)S(1)}, bf16[2,128,128]{2,1,0:T(8,128)(2,1)}, u32[]{:S(2)}) copy-start(bf16[2,128,128]{2,1,0:T(8,128)(2,1)} %param.17) | copy-start | bytes 196612
  46.8 13.1 %collective-permute-start.2 = (bf16[128,640]{1,0:T(8,128)(2,1)S(1)}, bf16[128,640]{1,0:T(8,128)(2,1)S(1)}, u32[]{:S(2)}, u32[]{:S(2)}) collective-permute-start(bf16[128,640]{1,0:T(8,128)(2,1)S(1)} %get-tuple-element.4.refs_0_), channel_id=1, source_target_pairs={{0,4},{4,0},{256,260},{260,256},{1,5},{5,1},{257,261},{261,257},{2... | collective-permute-start | bytes 491528 | tf_op jit(solution)/shard_map/ppermute | solution.py:43
  50.4 9.5 %collective-permute-start.3 = (bf16[128,640]{1,0:T(8,128)(2,1)S(1)}, bf16[128,640]{1,0:T(8,128)(2,1)S(1)}, u32[]{:S(2)}, u32[]{:S(2)}) collective-permute-start(bf16[128,640]{1,0:T(8,128)(2,1)S(1)} %get-tuple-element.4.refs_0_), channel_id=1, source_target_pairs={{0,256},{4,260},{256,0},{260,4},{1,257},{5,261},{257,1},{261,5},{2... | collective-permute-start | bytes 491528 | tf_op jit(solution)/shard_map/ppermute | solution.py:43
  55.1 10.6 %collective-permute-start.8 = (bf16[2,2,128,128]{3,2,1,0:T(8,128)(2,1)S(1)}, bf16[2,2,128,128]{3,2,1,0:T(8,128)(2,1)S(1)}, u32[]{:S(2)}, u32[]{:S(2)}) collective-permute-start(bf16[2,2,128,128]{3,2,1,0:T(8,128)(2,1)S(1)} %collective-permute-done.7.refs_3_), channel_id=1, source_target_pairs={{8,16},{16,8},{24,32},{32,24},{40,48},{48,40},{56,0},{0,56},{9,17}... | collective-permute-start | bytes 393224 | tf_op jit(solution)/shard_map/ppermute | solution.py:39
  66.5 13.0 %all-to-all-start.1 = ((bf16[4,2,2,128,128]{4,3,2,1,0:T(8,128)(2,1)}), bf16[4,2,2,128,128]{4,3,2,1,0:T(8,128)(2,1)S(1)}, u32[]{:S(2)}, u32[]{:S(2)}) async-start(bf16[4,2,2,128,128]{4,3,2,1,0:T(8,128)(2,1)} %shard_map.108), calls=%async_computation.1 | async-start | bytes 1048576 | tf_op jit(solution)/shard_map/all_to_all | solution.py:239
  72.1 30.0 %copy-start.7 = (bf16[2,128,128]{2,1,0:T(8,128)(2,1)S(1)}, bf16[2,128,128]{2,1,0:T(8,128)(2,1)}, u32[]{:S(2)}) copy-start(bf16[2,128,128]{2,1,0:T(8,128)(2,1)} %get-tuple-element.3.refs_6_) | copy-start | bytes 196612
  79.5 22.6 %all-to-all-start = ((bf16[4,6,2,128,128]{4,3,2,1,0:T(8,128)(2,1)}), bf16[4,6,2,128,128]{4,3,2,1,0:T(8,128)(2,1)S(1)}, u32[]{:S(2)}, u32[]{:S(2)}) async-start(bf16[4,6,2,128,128]{4,3,2,1,0:T(8,128)(2,1)} %shard_map.107), calls=%async_computation | async-start | bytes 3145728 | tf_op jit(solution)/shard_map/all_to_all | solution.py:236
  83.1 8.5 %collective-permute-start.4 = (bf16[128,640]{1,0:T(8,128)(2,1)S(1)}, bf16[128,640]{1,0:T(8,128)(2,1)S(1)}, u32[]{:S(2)}, u32[]{:S(2)}) collective-permute-start(bf16[128,640]{1,0:T(8,128)(2,1)S(1)} %get-tuple-element.4.refs_0_), channel_id=1, source_target_pairs={{0,260},{4,256},{256,4},{260,0},{1,261},{5,257},{257,5},{261,1},{2... | collective-permute-start | bytes 491528 | tf_op jit(solution)/shard_map/ppermute | solution.py:43
  102.1 25.9 %copy-start.1 = (bf16[640,1536]{1,0:T(8,128)(2,1)S(1)}, bf16[640,1536]{1,0:T(8,128)(2,1)}, u32[]{:S(2)}) copy-start(bf16[640,1536]{1,0:T(8,128)(2,1)} %w_ref.3) | copy-start | bytes 5898244

commit v4 on v3

--- a/solution.py
+++ b/solution.py
@@ -236,7 +236,7 @@
     near = lax.all_to_all(spread([own] + got, 4, gathered), "y", 0, 0)
     queries, fresh = project(gathered, modulate[None], w_query, w_kv)
     all_queries = [queries] + [flip(queries, bits) for bits in range(1, PEERS)]
-    far = lax.all_to_all(spread([swap(got[2], 1)], 4, all_queries[1], all_queries[2]), "y", 0, 0)
+    far = lax.all_to_all(spread([swap(got[2], 1)], 4, all_queries[1], all_queries[2], near), "y", 0, 0)
     where = jnp.stack([lax.axis_index(PLANE), 6 * lax.axis_index("y")]).astype(jnp.int32)
     partial = attend(where, all_queries, near, far, fresh)
     partial = lax.all_to_all(partial, PLANE, 0, 0)

time: 144 us -> 127 us (0.88)
  waiting for transfers between devices: 31.7 us -> 15.8 us
    all_to_all x1, waiting for transfers between devices: 10.6 us -> 0.01 us  [per_device(): near = lax.all_to_all(spread([own] + got, 4, gathered), 'y', 0, 0)]
    all_to_all x1, waiting for transfers between devices: 7.39 us -> 0.01 us  [per_device(): lax.all_to_all(spread([swap(got[2], 1)], 4, all_queries[1], all_queries[2...]
    unnamed x16 -> x18, local copies, waits for them, and re-layouts: 5.11 us -> 3.98 us
  transfers between devices with their start and end apart: 11 -> 11, of which waited for: 6 -> 5; matrix products, arithmetic and copies ran while one was open for 1% -> 1% of each run, Pallas kernels for 2% -> 1%
where the time goes in v4:
time: 127 us; the launch traced here: 126 us
  starting transfers between devices  48.6 us (38%)
  blocking collectives  37.5 us (30%)
  Pallas kernels  17.4 us (14%)
  waiting for transfers between devices  15.8 us (12%)
  local copies, waits for them, and re-layouts  4.74 us (4%)
  between operations  1.49 us (1%)
    ppermute x4, starting transfers between devices, swap(): return lax.ppermute(value, 'zh', pairs)  22.6 us
    all_to_all x1, blocking collectives, per_device(): partial = lax.all_to_all(partial, PLANE, 0, 0)  14 us
    ppermute x3, starting transfers between devices, flip(): return lax.ppermute(value, PLANE, [(i, i ^ bits) for i in range(PEERS)])  12.6 us
    pallas_call x1, Pallas kernels, attend(): pl.pallas_call(attend_kernel, in_specs=[pl.BlockSpec(memory_space=pltpu.S...  12.6 us
    all_to_all x1, blocking collectives, per_device(): terms = lax.all_to_all(terms, 'head', 0, 0)  12.5 us
    all_gather x1, blocking collectives, per_device(): gathered = lax.all_gather(stem, 'head', axis=1, tiled=True)  11 us
    ppermute x4, waiting for transfers between devices, swap(): return lax.ppermute(value, 'zh', pairs)  8.05 us
    ppermute x3, waiting for transfers between devices, flip(): return lax.ppermute(value, PLANE, [(i, i ^ bits) for i in range(PEERS)])  4.71 us
  transfers between devices with their start and end apart: 11, of which 5 were waited for; matrix products, arithmetic and copies ran while one was open for 1% of the time, Pallas kernels for 1%

profile of v4, /device:TPU:1, one launch (start us, length us, event | category | flops | bytes accessed | tf_op | source)
XLA Modules:
  0.0 126.3 jit_solution(5118724031994471339)
XLA Ops:
  0.6 5.7 %collective-permute-start.5 = (bf16[1,2,128,128]{3,2,1,0:T(8,128)(2,1)}, bf16[1,2,128,128]{3,2,1,0:T(8,128)(2,1)S(1)}, u32[]{:S(2)}, u32[]{:S(2)}) collective-permute-start(bf16[1,2,128,128]{3,2,1,0:T(8,128)(2,1)} %bitcast.13), channel_id=1, source_target_pairs={{0,8},{8,0},{16,24},{24,16},{32,40},{40,32},{48,56},{56,48},{1,9},... | collective-permute-start | bytes 196616 | tf_op jit(solution)/shard_map/ppermute | solution.py:39
  6.4 0.7 fusion.7
  7.1 3.5 %collective-permute-start = (bf16[1,384]{1,0:T(2,128)(2,1)S(1)}, bf16[1,384]{1,0:T(2,128)(2,1)S(1)}, u32[]{:S(2)}, u32[]{:S(2)}) collective-permute-start(bf16[1,384]{1,0:T(2,128)(2,1)S(1)} %get-tuple-element.7), channel_id=1, source_target_pairs={{0,4},{4,8},{8,12},{12,16},{16,20},{20,24},{24,28},{28,32},{32,36}... | collective-permute-start | bytes 2312 | tf_op jit(solution)/shard_map/ppermute | solution.py:227
  10.6 1.3 %collective-permute-start.1 = (bf16[1,384]{1,0:T(2,128)(2,1)S(1)}, bf16[1,384]{1,0:T(2,128)(2,1)S(1)}, u32[]{:S(2)}, u32[]{:S(2)}) collective-permute-start(bf16[1,384]{1,0:T(2,128)(2,1)S(1)} %get-tuple-element.6), channel_id=1, source_target_pairs={{4,0},{8,4},{12,8},{16,12},{20,16},{24,20},{28,24},{32,28},{36,32}... | collective-permute-start | bytes 2312 | tf_op jit(solution)/shard_map/ppermute | solution.py:228
  11.9 3.0 %collective-permute-done.1.after_ref = bf16[1,384]{1,0:T(2,128)(2,1)S(1)} collective-permute-done((bf16[1,384]{1,0:T(2,128)(2,1)S(1)}, bf16[1,384]{1,0:T(2,128)(2,1)S(1)}, u32[]{:S(2)}, u32[]{:S(2)}) %collective-permute-start.1) | collective-permute-done | bytes 800 | tf_op jit(solution)/shard_map/ppermute | solution.py:228
  14.9 0.9 copy-done.4
  15.8 0.7 copy-done.5
  16.5 0.1 shard_map.104.refs_2_
  16.6 0.8 copy-done.3
  17.5 8.9 %collective-permute-start.6 = (bf16[2,2,128,128]{3,2,1,0:T(8,128)(2,1)S(1)}, bf16[2,2,128,128]{3,2,1,0:T(8,128)(2,1)S(1)}, u32[]{:S(2)}, u32[]{:S(2)}) collective-permute-start(bf16[2,2,128,128]{3,2,1,0:T(8,128)(2,1)S(1)} %bitcast.16), channel_id=1, source_target_pairs={{8,16},{16,8},{24,32},{32,24},{40,48},{48,40},{56,0},{0,56},{9,17}... | collective-permute-start | bytes 393224 | tf_op jit(solution)/shard_map/ppermute | solution.py:39
  26.3 2.4 %collective-permute-done.6.refs_2_ = bf16[2,2,128,128]{3,2,1,0:T(8,128)(2,1)S(1)} collective-permute-done((bf16[2,2,128,128]{3,2,1,0:T(8,128)(2,1)S(1)}, bf16[2,2,128,128]{3,2,1,0:T(8,128)(2,1)S(1)}, u32[]{:S(2)}, u32[]{:S(2)}) %collective-permute-start.6) | collective-permute-done | bytes 131104 | tf_op jit(solution)/shard_map/ppermute | solution.py:39
  28.7 2.9 %collective-permute-start.7 = (bf16[2,2,128,128]{3,2,1,0:T(8,128)(2,1)S(1)}, bf16[2,2,128,128]{3,2,1,0:T(8,128)(2,1)S(1)}, u32[]{:S(2)}, u32[]{:S(2)}) collective-permute-start(bf16[2,2,128,128]{3,2,1,0:T(8,128)(2,1)S(1)} %collective-permute-done.6.refs_2_), channel_id=1, source_target_pairs={{0,8},{8,0},{16,24},{24,16},{32,40},{40,32},{48,56},{56,48},{1,9},... | collective-permute-start | bytes 393224 | tf_op jit(solution)/shard_map/ppermute | solution.py:39
  31.6 11.0 %all_gather.3.x_ref.refs_4_ = bf16[128,1536]{1,0:T(8,128)(2,1)S(1)} all-gather(bf16[128,384]{1,0:T(8,128)(2,1)S(1)} %shard_map.104.refs_2_), channel_id=1, replica_groups=mesh['xh'=2,'y'=4,'zh'=8,'zl'=2,'head'=4] {'head'}, dimensions={1}, use_global_device_ids=true | all-gather | bytes 491520 | tf_op jit(solution)/shard_map/all_gather | solution.py:233
  42.7 1.4 %shard_map.107 = bf16[4,6,2,128,128]{4,3,2,1,0:T(8,128)(2,1)} custom-call(bf16[1,2,128,128]{3,2,1,0:T(8,128)(2,1)S(1)} %bitcast.15, bf16[1,2,128,128]{3,2,1,0:T(8,128)(2,1)S(1)} %collective-permute-done.5.refs_1_, bf16[2,2,128,128]{3,2,1,0:T(8,128)(2,1)S(1)} %collective-permute-done.6.refs_2_, bf16[2,2,128,128]{3,2,1,0:T(8,128)(2,1)S(1)} %collective-permute-done.7.refs_3_, ...), custom_call_target="tpu_custom_call" | custom-call | flops 100000 | bytes 1000000 | tf_op jit(solution)/shard_map/pallas_call | solution.py:142
  44.0 4.3 %all-to-all-start = ((bf16[4,6,2,128,128]{4,3,2,1,0:T(8,128)(2,1)}), bf16[4,6,2,128,128]{4,3,2,1,0:T(8,128)(2,1)S(1)}, u32[]{:S(2)}, u32[]{:S(2)}) async-start(bf16[4,6,2,128,128]{4,3,2,1,0:T(8,128)(2,1)} %shard_map.107), calls=%async_computation | async-start | bytes 3145728 | tf_op jit(solution)/shard_map/all_to_all | solution.py:236
  49.1 1.5 %copy-done = bf16[1536,640]{1,0:T(8,128)(2,1)S(1)} copy-done((bf16[1536,640]{1,0:T(8,128)(2,1)S(1)}, bf16[1536,640]{1,0:T(8,128)(2,1)}, u32[]{:S(2)}) %copy-start) | copy-done | bytes 1966104
  50.7 1.4 %shard_map.105 = (bf16[128,640]{1,0:T(8,128)(2,1)S(1)}, bf16[2,128,128]{2,1,0:T(8,128)(2,1)}) custom-call(bf16[128,1536]{1,0:T(8,128)(2,1)S(1)} %all_gather.3.x_ref.refs_4_, f32[1,1536]{1,0:T(1,128)S(1)} %broadcast_in_dim.6.mod_ref, bf16[1536,640]{1,0:T(8,128)(2,1)S(1)} %copy-done, bf16[2,1536,128]{2,1,0:T(8,128)(2,1)S(1)} %copy-done.2), custom_call_target="tpu_custom_call" | custom-call | flops 400000000 | bytes 5000000 | tf_op jit(solution)/shard_map/pallas_call | solution.py:184
  52.1 4.9 %collective-permute-start.2 = (bf16[128,640]{1,0:T(8,128)(2,1)S(1)}, bf16[128,640]{1,0:T(8,128)(2,1)S(1)}, u32[]{:S(2)}, u32[]{:S(2)}) collective-permute-start(bf16[128,640]{1,0:T(8,128)(2,1)S(1)} %get-tuple-element.4.refs_0_), channel_id=1, source_target_pairs={{0,4},{4,0},{256,260},{260,256},{1,5},{5,1},{257,261},{261,257},{2... | collective-permute-start | bytes 491528 | tf_op jit(solution)/shard_map/ppermute | solution.py:43
  57.0 3.2 %collective-permute-start.3 = (bf16[128,640]{1,0:T(8,128)(2,1)S(1)}, bf16[128,640]{1,0:T(8,128)(2,1)S(1)}, u32[]{:S(2)}, u32[]{:S(2)}) collective-permute-start(bf16[128,640]{1,0:T(8,128)(2,1)S(1)} %get-tuple-element.4.refs_0_), channel_id=1, source_target_pairs={{0,256},{4,260},{256,0},{260,4},{1,257},{5,261},{257,1},{261,5},{2... | collective-permute-start | bytes 491528 | tf_op jit(solution)/shard_map/ppermute | solution.py:43
  60.2 5.1 %collective-permute-start.8 = (bf16[2,2,128,128]{3,2,1,0:T(8,128)(2,1)S(1)}, bf16[2,2,128,128]{3,2,1,0:T(8,128)(2,1)S(1)}, u32[]{:S(2)}, u32[]{:S(2)}) collective-permute-start(bf16[2,2,128,128]{3,2,1,0:T(8,128)(2,1)S(1)} %collective-permute-done.7.refs_3_), channel_id=1, source_target_pairs={{8,16},{16,8},{24,32},{32,24},{40,48},{48,40},{56,0},{0,56},{9,17}... | collective-permute-start | bytes 393224 | tf_op jit(solution)/shard_map/ppermute | solution.py:39
  65.4 0.1 collective-permute-done.3.refs_2_
  65.4 5.6 %collective-permute-done.8.refs_0_ = bf16[2,2,128,128]{3,2,1,0:T(8,128)(2,1)S(1)} collective-permute-done((bf16[2,2,128,128]{3,2,1,0:T(8,128)(2,1)S(1)}, bf16[2,2,128,128]{3,2,1,0:T(8,128)(2,1)S(1)}, u32[]{:S(2)}, u32[]{:S(2)}) %collective-permute-start.8) | collective-permute-done | bytes 131104 | tf_op jit(solution)/shard_map/ppermute | solution.py:39
  71.1 0.9 shard_map.108
  72.0 4.2 %all-to-all-start.1 = ((bf16[4,2,2,128,128]{4,3,2,1,0:T(8,128)(2,1)}), bf16[4,2,2,128,128]{4,3,2,1,0:T(8,128)(2,1)S(1)}, u32[]{:S(2)}, u32[]{:S(2)}) async-start(bf16[4,2,2,128,128]{4,3,2,1,0:T(8,128)(2,1)} %shard_map.108), calls=%async_computation.1 | async-start | bytes 1048576 | tf_op jit(solution)/shard_map/all_to_all | solution.py:239
  76.2 4.5 %collective-permute-start.4 = (bf16[128,640]{1,0:T(8,128)(2,1)S(1)}, bf16[128,640]{1,0:T(8,128)(2,1)S(1)}, u32[]{:S(2)}, u32[]{:S(2)}) collective-permute-start(bf16[128,640]{1,0:T(8,128)(2,1)S(1)} %get-tuple-element.4.refs_0_), channel_id=1, source_target_pairs={{0,260},{4,256},{256,4},{260,0},{1,261},{5,257},{257,5},{261,1},{2... | collective-permute-start | bytes 491528 | tf_op jit(solution)/shard_map/ppermute | solution.py:43
  80.7 0.1 pad_add_fusion.where_ref
  80.8 4.6 %collective-permute-done.4.refs_3_ = bf16[128,640]{1,0:T(8,128)(2,1)S(1)} collective-permute-done((bf16[128,640]{1,0:T(8,128)(2,1)S(1)}, bf16[128,640]{1,0:T(8,128)(2,1)S(1)}, u32[]{:S(2)}, u32[]{:S(2)}) %collective-permute-start.4) | collective-permute-done | bytes 163872 | tf_op jit(solution)/shard_map/ppermute | solution.py:43
  85.5 12.6 %shard_map.109 = bf16[4,128,768]{2,1,0:T(8,128)(2,1)S(1)} custom-call(s32[2]{0:T(128)S(1)} %pad_add_fusion.where_ref, bf16[128,640]{1,0:T(8,128)(2,1)S(1)} %get-tuple-element.4.refs_0_, bf16[128,640]{1,0:T(8,128)(2,1)S(1)} %collective-permute-done.2.refs_1_, bf16[128,640]{1,0:T(8,128)(2,1)S(1)} %collective-permute-done.3.refs_2_, ...), custom_call_target="tpu_custom_call" | custom-call | flops 15000000512 | bytes 4000000 | tf_op jit(solution)/shard_map/pallas_call | solution.py:112
  98.0 14.0 %all_to_all.20.parts_ref = bf16[4,128,768]{2,1,0:T(8,128)(2,1)S(1)} all-to-all(bf16[4,128,768]{2,1,0:T(8,128)(2,1)S(1)} %shard_map.109), channel_id=1, replica_groups=mesh['xh'=2,'y'=4,'zh'=8,'zl'=2,'head'=4] {'xh','zl'}, dimensions={0} | all-to-all | bytes 1572864 | tf_op jit(solution)/shard_map/all_to_all | solution.py:242
  112.0 1.1 shard_map.110
  113.2 12.5 %all_to_all.21 = bf16[4,128,384]{2,1,0:T(8,128)(2,1)S(1)} all-to-all(bf16[4,128,384]{2,1,0:T(8,128)(2,1)S(1)} %bitcast.17), channel_id=1, replica_groups=mesh['xh'=2,'y'=4,'zh'=8,'zl'=2,'head'=4] {'head'}, dimensions={0} | all-to-all | bytes 786432 | tf_op jit(solution)/shard_map/all_to_all | solution.py:245
  125.7 0.7 add_convert_fusion
  (25 shorter events, 0.2 us)
Async XLA Ops:
  0.6 16.0 %collective-permute-start.5 = (bf16[1,2,128,128]{3,2,1,0:T(8,128)(2,1)}, bf16[1,2,128,128]{3,2,1,0:T(8,128)(2,1)S(1)}, u32[]{:S(2)}, u32[]{:S(2)}) collective-permute-start(bf16[1,2,128,128]{3,2,1,0:T(8,128)(2,1)} %bitcast.13), channel_id=1, source_target_pairs={{0,8},{8,0},{16,24},{24,16},{32,40},{40,32},{48,56},{56,48},{1,9},... | collective-permute-start | bytes 196616 | tf_op jit(solution)/shard_map/ppermute | solution.py:39
  7.1 4.8 %collective-permute-start = (bf16[1,384]{1,0:T(2,128)(2,1)S(1)}, bf16[1,384]{1,0:T(2,128)(2,1)S(1)}, u32[]{:S(2)}, u32[]{:S(2)}) collective-permute-start(bf16[1,384]{1,0:T(2,128)(2,1)S(1)} %get-tuple-element.7), channel_id=1, source_target_pairs={{0,4},{4,8},{8,12},{12,16},{16,20},{20,24},{24,28},{28,32},{32,36}... | collective-permute-start | bytes 2312 | tf_op jit(solution)/shard_map/ppermute | solution.py:227
  10.6 4.3 %collective-permute-start.1 = (bf16[1,384]{1,0:T(2,128)(2,1)S(1)}, bf16[1,384]{1,0:T(2,128)(2,1)S(1)}, u32[]{:S(2)}, u32[]{:S(2)}) collective-permute-start(bf16[1,384]{1,0:T(2,128)(2,1)S(1)} %get-tuple-element.6), channel_id=1, source_target_pairs={{4,0},{8,4},{12,8},{16,12},{20,16},{24,20},{28,24},{32,28},{36,32}... | collective-permute-start | bytes 2312 | tf_op jit(solution)/shard_map/ppermute | solution.py:228
  14.9 0.9 copy-start.4
  15.8 0.7 copy-start.5
  16.6 0.8 copy-start.3
  17.5 11.3 %collective-permute-start.6 = (bf16[2,2,128,128]{3,2,1,0:T(8,128)(2,1)S(1)}, bf16[2,2,128,128]{3,2,1,0:T(8,128)(2,1)S(1)}, u32[]{:S(2)}, u32[]{:S(2)}) collective-permute-start(bf16[2,2,128,128]{3,2,1,0:T(8,128)(2,1)S(1)} %bitcast.16), channel_id=1, source_target_pairs={{8,16},{16,8},{24,32},{32,24},{40,48},{48,40},{56,0},{0,56},{9,17}... | collective-permute-start | bytes 393224 | tf_op jit(solution)/shard_map/ppermute | solution.py:39
  28.7 13.9 %collective-permute-start.7 = (bf16[2,2,128,128]{3,2,1,0:T(8,128)(2,1)S(1)}, bf16[2,2,128,128]{3,2,1,0:T(8,128)(2,1)S(1)}, u32[]{:S(2)}, u32[]{:S(2)}) collective-permute-start(bf16[2,2,128,128]{3,2,1,0:T(8,128)(2,1)S(1)} %collective-permute-done.6.refs_2_), channel_id=1, source_target_pairs={{0,8},{8,0},{16,24},{24,16},{32,40},{40,32},{48,56},{56,48},{1,9},... | collective-permute-start | bytes 393224 | tf_op jit(solution)/shard_map/ppermute | solution.py:39
  44.0 5.0 %copy-start.7 = (f32[1536]{0:T(1024)S(1)}, f32[1536]{0:T(1024)}, u32[]{:S(2)}) copy-start(f32[1536]{0:T(1024)} %param.12) | copy-start | bytes 18436
  44.0 5.0 %copy-start.8 = (f32[1536]{0:T(1024)S(1)}, f32[1536]{0:T(1024)}, u32[]{:S(2)}) copy-start(f32[1536]{0:T(1024)} %param.13) | copy-start | bytes 18436
  44.0 5.1 %copy-start.2 = (bf16[2,1536,128]{2,1,0:T(8,128)(2,1)S(1)}, bf16[2,1536,128]{2,1,0:T(8,128)(2,1)}, u32[]{:S(2)}) copy-start(bf16[2,1536,128]{2,1,0:T(8,128)(2,1)} %wkv_ref.1) | copy-start | bytes 2359300
  44.0 27.1 %all-to-all-start = ((bf16[4,6,2,128,128]{4,3,2,1,0:T(8,128)(2,1)}), bf16[4,6,2,128,128]{4,3,2,1,0:T(8,128)(2,1)S(1)}, u32[]{:S(2)}, u32[]{:S(2)}) async-start(bf16[4,6,2,128,128]{4,3,2,1,0:T(8,128)(2,1)} %shard_map.107), calls=%async_computation | async-start | bytes 3145728 | tf_op jit(solution)/shard_map/all_to_all | solution.py:236
  49.1 1.5 %copy-start = (bf16[1536,640]{1,0:T(8,128)(2,1)S(1)}, bf16[1536,640]{1,0:T(8,128)(2,1)}, u32[]{:S(2)}) copy-start(bf16[1536,640]{1,0:T(8,128)(2,1)} %wq_ref.1) | copy-start | bytes 5898244
  52.1 33.4 %copy-start.6 = (bf16[2,128,128]{2,1,0:T(8,128)(2,1)S(1)}, bf16[2,128,128]{2,1,0:T(8,128)(2,1)}, u32[]{:S(2)}) copy-start(bf16[2,128,128]{2,1,0:T(8,128)(2,1)} %get-tuple-element.3.refs_6_) | copy-start | bytes 196612
  52.1 13.3 %collective-permute-start.2 = (bf16[128,640]{1,0:T(8,128)(2,1)S(1)}, bf16[128,640]{1,0:T(8,128)(2,1)S(1)}, u32[]{:S(2)}, u32[]{:S(2)}) collective-permute-start(bf16[128,640]{1,0:T(8,128)(2,1)S(1)} %get-tuple-element.4.refs_0_), channel_id=1, source_target_pairs={{0,4},{4,0},{256,260},{260,256},{1,5},{5,1},{257,261},{261,257},{2... | collective-permute-start | bytes 491528 | tf_op jit(solution)/shard_map/ppermute | solution.py:43
  57.0 8.4 %collective-permute-start.3 = (bf16[128,640]{1,0:T(8,128)(2,1)S(1)}, bf16[128,640]{1,0:T(8,128)(2,1)S(1)}, u32[]{:S(2)}, u32[]{:S(2)}) collective-permute-start(bf16[128,640]{1,0:T(8,128)(2,1)S(1)} %get-tuple-element.4.refs_0_), channel_id=1, source_target_pairs={{0,256},{4,260},{256,0},{260,4},{1,257},{5,261},{257,1},{261,5},{2... | collective-permute-start | bytes 491528 | tf_op jit(solution)/shard_map/ppermute | solution.py:43
  60.2 10.9 %collective-permute-start.8 = (bf16[2,2,128,128]{3,2,1,0:T(8,128)(2,1)S(1)}, bf16[2,2,128,128]{3,2,1,0:T(8,128)(2,1)S(1)}, u32[]{:S(2)}, u32[]{:S(2)}) collective-permute-start(bf16[2,2,128,128]{3,2,1,0:T(8,128)(2,1)S(1)} %collective-permute-done.7.refs_3_), channel_id=1, source_target_pairs={{8,16},{16,8},{24,32},{32,24},{40,48},{48,40},{56,0},{0,56},{9,17}... | collective-permute-start | bytes 393224 | tf_op jit(solution)/shard_map/ppermute | solution.py:39
  72.0 13.5 %all-to-all-start.1 = ((bf16[4,2,2,128,128]{4,3,2,1,0:T(8,128)(2,1)}), bf16[4,2,2,128,128]{4,3,2,1,0:T(8,128)(2,1)S(1)}, u32[]{:S(2)}, u32[]{:S(2)}) async-start(bf16[4,2,2,128,128]{4,3,2,1,0:T(8,128)(2,1)} %shard_map.108), calls=%async_computation.1 | async-start | bytes 1048576 | tf_op jit(solution)/shard_map/all_to_all | solution.py:239
  76.2 9.2 %collective-permute-start.4 = (bf16[128,640]{1,0:T(8,128)(2,1)S(1)}, bf16[128,640]{1,0:T(8,128)(2,1)S(1)}, u32[]{:S(2)}, u32[]{:S(2)}) collective-permute-start(bf16[128,640]{1,0:T(8,128)(2,1)S(1)} %get-tuple-element.4.refs_0_), channel_id=1, source_target_pairs={{0,260},{4,256},{256,4},{260,0},{1,261},{5,257},{257,5},{261,1},{2... | collective-permute-start | bytes 491528 | tf_op jit(solution)/shard_map/ppermute | solution.py:43
  85.5 26.6 %copy-start.1 = (bf16[640,1536]{1,0:T(8,128)(2,1)S(1)}, bf16[640,1536]{1,0:T(8,128)(2,1)}, u32[]{:S(2)}) copy-start(bf16[640,1536]{1,0:T(8,128)(2,1)} %w_ref.3) | copy-start | bytes 5898244
